TPU v7x, 256 devices: a whole 4x4x8 slice. The times are simulated.
256 devices in a mesh: dp: 32 (over x, z), codebook: 8 (over y, core).
Axes of the slice: x: 4, y: 4, z: 8, core: 2. Of those that a mesh axis runs over, the one named last changes fastest.
Arguments:
- keys: bfloat16 [32768, 128], P('dp'), may hold values from -25 to 25
- codebook: bfloat16 [65536, 128], P(('dp', 'codebook')), may hold values from -6 to 6
Outputs:
- new_codebook: bfloat16 [65536, 128], P(('dp', 'codebook'))
- loglik: float32 [32768], P('dp')
All inputs are finite; a program needn't handle non-finite values.
Results may differ from a plain program's by a relative error of at most 0.008.
Values may be sent and summed in bfloat16 or wider, within the bound.
A program may use at most 64 MiB of HBM per device.

v0:
```python
import jax
import jax.numpy as jnp
from jax import lax
from jax.sharding import PartitionSpec as P

BETA = 0.1


def scores_of(keys, sq_key, block):
    cross = jnp.dot(keys, block.T, preferred_element_type=jnp.float32)
    block_f = block.astype(jnp.float32)
    sq_code = jnp.sum(block_f * block_f, axis=1)
    return BETA * (2.0 * cross - sq_key[:, None] - sq_code[None, :])


def local(keys, codebook):
    local_entries = lax.all_gather(codebook, "dp", axis=0, tiled=True)
    count = local_entries.shape[0]
    width = min(1024, count)
    blocks = local_entries.reshape(count // width, width, keys.shape[1])
    keys_f = keys.astype(jnp.float32)
    sq_key = jnp.sum(keys_f * keys_f, axis=1)

    def block_stats(block):
        score = scores_of(keys, sq_key, block)
        upper = jnp.max(score, axis=1)
        return (upper, jnp.sum(jnp.exp(score - upper[:, None]), axis=1))

    maxima, totals = lax.map(block_stats, blocks)
    peak_local = jnp.max(maxima, axis=0)
    total_local = jnp.sum(totals * jnp.exp(maxima - peak_local[None, :]), axis=0)
    peak = lax.pmax(peak_local, "codebook")
    total = lax.psum(total_local * jnp.exp(peak_local - peak), "codebook")
    loglik = peak + jnp.log(total)

    def accumulate(block):
        score = scores_of(keys, sq_key, block)
        resp = jnp.exp(score - loglik[:, None]).astype(jnp.bfloat16)
        weighted = lax.dot_general(
            resp, keys, (((0,), (0,)), ((), ())), preferred_element_type=jnp.float32
        )
        mass = jnp.sum(resp.astype(jnp.float32), axis=0)
        return (weighted, mass)

    weighted, mass = lax.map(accumulate, blocks)
    weighted = weighted.reshape(count, keys.shape[1])
    mass = mass.reshape(count)
    owned = codebook.shape[0]
    weighted, mass = lax.psum((weighted, mass), "dp")
    offset = lax.axis_index("dp") * owned
    weighted = lax.dynamic_slice_in_dim(weighted, offset, owned, 0)
    mass = lax.dynamic_slice_in_dim(mass, offset, owned, 0)
    new_codebook = ((weighted + codebook.astype(jnp.float32)) / (mass + 1.0)[:, None]).astype(
        jnp.bfloat16
    )
    return (new_codebook, loglik)


def solution(mesh):
    placed = (P("dp", None), P(("dp", "codebook"), None))
    return jax.shard_map(
        local,
        mesh=mesh,
        in_specs=placed,
        out_specs=(P(("dp", "codebook"), None), P("dp")),
        check_vma=False,
    )
```

profile of v0, /device:TPU:1, one launch (start us, length us, event | category | flops | bytes accessed | tf_op | source)
XLA Modules:
  0.0 361.0 jit_solution(15930573332251830116)
XLA Ops:
  8.0 1.2 multiply_reduce_fusion.2
  9.1 79.3 %all-gather.2.cloned.1.call-done = bf16[8192,128]{1,0:T(8,128)(2,1)} async-done(((bf16[256,128]{1,0:T(8,128)(2,1)}), bf16[8192,128]{1,0:T(8,128)(2,1)}) %all-gather.2.cloned.1.call-update) | async-done | bytes 2097168 | tf_op jit(solution)/shard_map/all_gather | solution.py:17
  88.4 36.0 %while.24 = (s32[]{:T(128)}, f32[8,1024]{1,0:T(8,128)S(1)}, f32[8,1024]{1,0:T(8,128)S(1)}, bf16[8,1024,128]{2,1,0:T(8,128)(2,1)}, bf16[1024,128]{1,0:T(8,128)(2,1)}, /*index=5*/f32[1024]{0:T(1024)S(1)}, s32[]{:T(128)}, s32[]{:T(128)}) while((s32[]{:T(128)}, f32[8,1024]{1,0:T(8,128)S(1)}, f32[8,1024]{1,0:T(8,128)S(1)}, ...), condition=%wide.region_5.6_spmd, body=%wide.region_1.5_spmd.sunk | while | flops 280359936 | bytes 9224301 | solution.py:29
  89.6 1.9 fusion.20
  92.9 1.2 multiply_reduce_fusion.6
  94.1 1.9 fusion.20
  97.4 1.2 multiply_reduce_fusion.6
  98.6 1.9 fusion.20
  101.9 1.2 multiply_reduce_fusion.6
  103.1 1.9 fusion.20
  106.4 1.2 multiply_reduce_fusion.6
  107.6 1.9 fusion.20
  110.9 1.2 multiply_reduce_fusion.6
  112.1 1.9 fusion.20
  115.4 1.2 multiply_reduce_fusion.6
  116.6 1.9 fusion.20
  119.9 1.2 multiply_reduce_fusion.6
  121.1 1.9 fusion.20
  124.4 16.3 %pmax.7 = f32[1024]{0:T(1024)S(1)} all-reduce(f32[1024]{0:T(1024)S(1)} %reduce_max.18), channel_id=1, replica_groups=mesh['dp'=32,'codebook'=8] {'codebook'}, use_global_device_ids=true, to_apply=%region_7.8 | all-reduce | flops 1024 | bytes 8192 | tf_op jit(solution)/shard_map/pmax | solution.py:32
  140.8 12.4 %psum.21 = f32[1024]{0:T(1024)S(1)} all-reduce(f32[1024]{0:T(1024)S(1)} %exponential_multiply_fusion), channel_id=1, replica_groups=mesh['dp'=32,'codebook'=8] {'codebook'}, use_global_device_ids=true, to_apply=%region_9.10 | all-reduce | flops 1024 | bytes 8192 | tf_op jit(solution)/shard_map/psum | solution.py:33
  153.2 42.4 %while.25 = (s32[]{:T(128)}, f32[8,1024,128]{2,1,0:T(8,128)}, f32[8,1024]{1,0:T(8,128)S(1)}, bf16[8,1024,128]{2,1,0:T(8,128)(2,1)}, bf16[1024,128]{1,0:T(8,128)(...) while((s32[]{:T(128)}, f32[8,1024,128]{2,1,0:T(8,128)}, ...), condition=%wide.region_13.14_spmd, body=%wide.region_10.13_spmd.sunk | while | flops 545650688 | bytes 6844561 | solution.py:45
  153.3 1.2 multiply_reduce_fusion.7
  154.5 2.4 convert_reduce_fusion.2
  157.0 1.5 fusion.24
  158.5 1.2 multiply_reduce_fusion.7
  159.7 2.4 convert_reduce_fusion.2
  162.3 1.6 fusion.24
  163.8 1.2 multiply_reduce_fusion.7
  165.0 2.4 convert_reduce_fusion.2
  167.6 1.6 fusion.24
  169.1 1.2 multiply_reduce_fusion.7
  170.4 2.4 convert_reduce_fusion.2
  172.9 1.6 fusion.24
  174.4 1.2 multiply_reduce_fusion.7
  175.7 2.4 convert_reduce_fusion.2
  178.2 1.5 fusion.24
  179.7 1.2 multiply_reduce_fusion.7
  180.9 2.4 convert_reduce_fusion.2
  183.5 1.6 fusion.24
  185.0 1.2 multiply_reduce_fusion.7
  186.2 2.4 convert_reduce_fusion.2
  188.8 1.5 fusion.24
  190.3 1.2 multiply_reduce_fusion.7
  191.5 2.4 convert_reduce_fusion.2
  194.1 1.6 fusion.24
  195.7 112.8 %psum.23 = f32[8192]{0:T(1024)S(1)} all-reduce(f32[8192]{0:T(1024)S(1)} %bitcast.58), channel_id=1, replica_groups=mesh['dp'=32,'codebook'=8] {'dp'}, use_global_device_ids=true, to_apply=%region_15.16 | all-reduce | flops 8192 | bytes 65536 | tf_op jit(solution)/shard_map/psum | solution.py:49
  308.5 44.0 %all-reduce.2.cloned.1.call-done = f32[8192,128]{1,0:T(8,128)} async-done(((f32[8192,128]{1,0:T(8,128)}), f32[8192,128]{1,0:T(8,128)}) %all-reduce.2.cloned.1.call-update) | async-done | bytes 4194320 | tf_op jit(solution)/shard_map/psum | solution.py:49
  352.5 1.6 divide_convert_fusion
  (67 shorter events, 13.9 us)
Async XLA Ops:
  7.2 81.2 %all-gather.2.cloned.1.call-start = ((), (), s32[]{:S(2)}) async-start(), calls=%async_computation | async-start | bytes 2162688 | tf_op jit(solution)/shard_map/all_gather | solution.py:17
  7.9 344.6 %all-reduce.2.cloned.1.call-start = ((), (), s32[]{:S(2)}) async-start(), calls=%async_computation.1 | async-start | bytes 8388608 | tf_op jit(solution)/shard_map/psum | solution.py:49
  153.2 3.8 %copy-start = (bf16[1024,128]{1,0:T(8,128)(2,1)S(1)}, bf16[1024,128]{1,0:T(8,128)(2,1)}, u32[]{:S(2)}) copy-start(bf16[1024,128]{1,0:T(8,128)(2,1)} %get-tuple-element.241) | copy-start | bytes 786436 | tf_op jit(solution)/shard_map/while
  158.5 3.7 %copy-start = (bf16[1024,128]{1,0:T(8,128)(2,1)S(1)}, bf16[1024,128]{1,0:T(8,128)(2,1)}, u32[]{:S(2)}) copy-start(bf16[1024,128]{1,0:T(8,128)(2,1)} %get-tuple-element.241) | copy-start | bytes 786436 | tf_op jit(solution)/shard_map/while
  163.8 3.7 %copy-start = (bf16[1024,128]{1,0:T(8,128)(2,1)S(1)}, bf16[1024,128]{1,0:T(8,128)(2,1)}, u32[]{:S(2)}) copy-start(bf16[1024,128]{1,0:T(8,128)(2,1)} %get-tuple-element.241) | copy-start | bytes 786436 | tf_op jit(solution)/shard_map/while
  169.1 3.7 %copy-start = (bf16[1024,128]{1,0:T(8,128)(2,1)S(1)}, bf16[1024,128]{1,0:T(8,128)(2,1)}, u32[]{:S(2)}) copy-start(bf16[1024,128]{1,0:T(8,128)(2,1)} %get-tuple-element.241) | copy-start | bytes 786436 | tf_op jit(solution)/shard_map/while
  174.4 3.7 %copy-start = (bf16[1024,128]{1,0:T(8,128)(2,1)S(1)}, bf16[1024,128]{1,0:T(8,128)(2,1)}, u32[]{:S(2)}) copy-start(bf16[1024,128]{1,0:T(8,128)(2,1)} %get-tuple-element.241) | copy-start | bytes 786436 | tf_op jit(solution)/shard_map/while
  179.7 3.7 %copy-start = (bf16[1024,128]{1,0:T(8,128)(2,1)S(1)}, bf16[1024,128]{1,0:T(8,128)(2,1)}, u32[]{:S(2)}) copy-start(bf16[1024,128]{1,0:T(8,128)(2,1)} %get-tuple-element.241) | copy-start | bytes 786436 | tf_op jit(solution)/shard_map/while
  185.0 3.7 %copy-start = (bf16[1024,128]{1,0:T(8,128)(2,1)S(1)}, bf16[1024,128]{1,0:T(8,128)(2,1)}, u32[]{:S(2)}) copy-start(bf16[1024,128]{1,0:T(8,128)(2,1)} %get-tuple-element.241) | copy-start | bytes 786436 | tf_op jit(solution)/shard_map/while
  190.3 3.7 %copy-start = (bf16[1024,128]{1,0:T(8,128)(2,1)S(1)}, bf16[1024,128]{1,0:T(8,128)(2,1)}, u32[]{:S(2)}) copy-start(bf16[1024,128]{1,0:T(8,128)(2,1)} %get-tuple-element.241) | copy-start | bytes 786436 | tf_op jit(solution)/shard_map/while
  195.6 158.6 %copy-start.2 = (f32[1024]{0:T(1024)}, f32[1024]{0:T(1024)S(1)}, u32[]{:S(2)}) copy-start(f32[1024]{0:T(1024)S(1)} %get-tuple-element.256) | copy-start | bytes 12292
  195.6 156.9 %copy-start.1 = (bf16[256,128]{1,0:T(8,128)(2,1)S(1)}, bf16[256,128]{1,0:T(8,128)(2,1)}, u32[]{:S(2)}) copy-start(bf16[256,128]{1,0:T(8,128)(2,1)} %param.7) | copy-start | bytes 196612
Sparse Core Ops, SparseCore 0:
  10.6 77.7 all-gather.1
  195.8 156.7 all-reduce.1
where the time goes:
time: 364 us; the launch traced here: 361 us
  blocking collectives  142 us (39%)
  waiting for transfers between devices  124 us (34%)
  matrix products  46.9 us (13%)
  other arithmetic  31.1 us (9%)
  between operations  14.1 us (4%)
    psum x1, blocking collectives, local(): weighted, mass = lax.psum((weighted, mass), 'dp')  113 us
    all_gather x1, waiting for transfers between devices, local(): local_entries = lax.all_gather(codebook, 'dp', axis=0, tiled=True)  79.3 us
    psum x1, waiting for transfers between devices, local(): weighted, mass = lax.psum((weighted, mass), 'dp')  44 us
    dot_general x16, matrix products, scores_of(): cross = jnp.dot(keys, block.T, preferred_element_type=jnp.float32)  34.5 us
    reduce_sum x16, other arithmetic, scores_of(): sq_code = jnp.sum(block_f * block_f, axis=1)  18.9 us
    pmax x1, blocking collectives, local(): peak = lax.pmax(peak_local, 'codebook')  16.3 us
    psum x1, blocking collectives, local(): total = lax.psum(total_local * jnp.exp(peak_local - peak), 'codebook')  12.4 us
    dot_general x8, matrix products, accumulate(): lax.dot_general(resp, keys, (((0,), (0,)), ((), ())), preferred_element_t...  12.4 us
  transfers between devices with their start and end apart: 2, of which 2 were waited for; matrix products, arithmetic and copies ran while one was open for 0% of the time, Pallas kernels for 0%

commit v1 on v0

v1 whole, which is shorter than its diff:
```python
import jax
import jax.numpy as jnp
from jax import lax
from jax.experimental import pallas as pl
from jax.experimental.pallas import tpu as pltpu
from jax.sharding import PartitionSpec as P

MESH = pl.DeviceIdType.MESH
NX, NZ, NY = 4, 8, 4
TOK, OWN, E = 1024, 256, 128
TILE = 256
BETA = 0.1
LOG2E = 1.4426950408889634
LN2 = 0.6931471805599453
ALPHA = 2.0 * BETA * LOG2E
NT = (((1,), (1,)), ((), ()))


def ring_order(o, n):
    k = (o + 1) // 2
    odd = o % 2
    return (odd * k + (1 - odd) * (n - k)) % n


def to_tile(row):
    return jnp.concatenate([row[:, 128 * r : 128 * (r + 1)] for r in range(8)], axis=0)


def to_row(tile):
    return jnp.concatenate([tile[r : r + 1, :] for r in range(8)], axis=1)


def kernel(
    keys, code, new_code, loglik,
    kt, cb, aug, prob, top, tot, scale, kst, stats, acc, wsend, wrecv,
    key_send, key_recv, core_send, core_recv, code_send, code_recv,
    stat_send, stat_recv, sum_send, sum_recv,
):
    dp, col = lax.axis_index("dp"), lax.axis_index("codebook")
    x, z = dp // NZ, dp % NZ
    y, core = col // 2, col % 2

    def at(dx=0, dz=0, dy=0, dc=0):
        return (
            lax.rem(x + dx, NX) * NZ + lax.rem(z + dz, NZ),
            lax.rem(y + dy, NY) * 2 + lax.rem(core + dc, 2),
        )

    def plane(r):
        return at(dx=r // 8, dy=(r // 2) % 4, dc=r % 2)

    barrier = pltpu.get_barrier_semaphore()

    def greet_plane(r, carry):
        pl.semaphore_signal(barrier, inc=1, device_id=plane(r), device_id_type=MESH)
        return carry

    def greet_ring(d, carry):
        pl.semaphore_signal(barrier, inc=1, device_id=at(dz=d), device_id_type=MESH)
        return carry

    lax.fori_loop(1, 32, greet_plane, 0)
    lax.fori_loop(1, NZ, greet_ring, 0)

    cb[0] = code[...]
    kt[0, :E, :] = keys[...].astype(jnp.float32).T.astype(jnp.bfloat16)
    row = lax.broadcasted_iota(jnp.int32, (E, TOK), 0)
    ones = jnp.where(row < 3, 1.0, 0.0).astype(jnp.bfloat16)
    for i in range(NX):
        kt[i, E:, :] = ones
    kst[:, E:, :] = jnp.zeros((2, E, TOK), jnp.bfloat16)
    half = pl.ds(pl.multiple_of(core * (E // 2), E // 2), E // 2)

    pl.semaphore_wait(barrier, 31 + NZ - 1)

    def key_copy(p):
        to = (NX - ring_order(p, NX)) % NX
        return pltpu.make_async_remote_copy(
            src_ref=kt.at[0, half], dst_ref=kt.at[p, half],
            send_sem=key_send.at[p], recv_sem=key_recv.at[p],
            device_id=at(dx=to), device_id_type=MESH,
        )

    def code_copy(o):
        to = (NZ - ring_order(o, NZ)) % NZ
        return pltpu.make_async_remote_copy(
            src_ref=code, dst_ref=cb.at[o],
            send_sem=code_send.at[o], recv_sem=code_recv.at[o],
            device_id=at(dz=to), device_id_type=MESH,
        )

    def core_copy(p):
        return pltpu.make_async_remote_copy(
            src_ref=kt.at[p, half], dst_ref=kt.at[p, half],
            send_sem=core_send.at[p], recv_sem=core_recv.at[p],
            device_id=at(dc=1), device_id_type=MESH,
        )

    for p in range(1, NX):
        key_copy(p).start()
    for o in range(1, NZ):
        code_copy(o).start()

    def prepare(o):
        c = cb[o].astype(jnp.float32)
        h = -0.5 * jnp.sum(c * c, axis=1, keepdims=True)
        hi = h.astype(jnp.bfloat16).astype(jnp.float32)
        mid = (h - hi).astype(jnp.bfloat16).astype(jnp.float32)
        lo = h - hi - mid
        lane = lax.broadcasted_iota(jnp.int32, (OWN, E), 1)
        both = jnp.where(lane == 0, hi, jnp.where(lane == 1, mid, lo))
        aug[o] = jnp.where(lane < 3, both, 0.0).astype(jnp.bfloat16)

    def unit(i, o):
        c = jnp.concatenate([cb[o], aug[o]], axis=1)
        n = TOK // TILE

        def cross(q):
            k = kt[i, :, q * TILE : (q + 1) * TILE]
            return jnp.dot(c, k, preferred_element_type=jnp.float32)

        s = cross(0)
        for q in range(n):
            later = cross(q + 1) if q + 1 < n else None
            m = jnp.max(s, axis=0, keepdims=True)
            p = jnp.exp2((s - m) * ALPHA)
            span = slice(q * TILE, (q + 1) * TILE)
            top[i, pl.ds(o, 1), span] = m
            tot[i, pl.ds(o, 1), span] = jnp.sum(p, axis=0, keepdims=True)
            prob[i * NZ + o, :, span] = p.astype(jnp.bfloat16)
            s = later

    def arrive(o):
        code_copy(o).wait_recv()
        prepare(o)

    def first(o, carry):
        @pl.when(o > 0)
        def _():
            arrive(o)

        unit(0, o)
        return carry

    def near(n, carry):
        unit(1 + n // 5, n % 5)
        return carry

    def far(n, carry):
        @pl.when(n % 3 == 0)
        def _():
            arrive(5 + n // 3)

        unit(n % 3, 5 + n // 3)
        return carry

    def last(o, carry):
        unit(3, o)
        return carry

    def stat_copy(i, r):
        away = (ring_order(i, NX) + NX - r // 8) % NX
        slot = away + away // 2 - 2 * (away // 3)
        return pltpu.make_async_remote_copy(
            src_ref=stats.at[i, 0], dst_ref=stats.at[slot, r],
            send_sem=stat_send.at[i], recv_sem=stat_recv.at[slot],
            device_id=plane(r), device_id_type=MESH,
        )

    def local_sum(i):
        m = top[i]
        peak = jnp.max(m, axis=0, keepdims=True)
        total = jnp.sum(tot[i] * jnp.exp2((m - peak) * ALPHA), axis=0, keepdims=True)
        stats[i, 0] = to_tile(ALPHA * peak + jnp.log2(total))

    def send_stats(i):
        local_sum(i)

        def go(r, carry):
            stat_copy(i, r).start()
            return carry

        lax.fori_loop(1, 32, go, 0)

    def all_stats(i):
        return pltpu.make_async_remote_copy(
            src_ref=stats.at[i, pl.ds(1, 31)], dst_ref=stats.at[i, pl.ds(1, 31)],
            send_sem=stat_send.at[i], recv_sem=stat_recv.at[i],
            device_id=at(dc=1), device_id_type=MESH,
        )

    def finish_stats(i):
        all_stats(i).wait_recv()
        v = stats[i]
        peak = jnp.max(v, axis=0)
        lse = peak + jnp.log2(jnp.sum(jnp.exp2(v - peak[None]), axis=0))
        if i == 0:
            k = kt[0, :E, :].astype(jnp.float32)
            sq = to_tile(jnp.sum(k * k, axis=0, keepdims=True))
            loglik[...] = LN2 * lse - BETA * sq
        scale[i] = jnp.exp2(ALPHA * top[i] - to_row(lse))

    def weigh(i, o):
        f = scale[i, pl.ds(o, 1), :]
        b = i % 2
        kst[b, :E, :] = (kt[i, :E, :].astype(jnp.float32) * f).astype(jnp.bfloat16)
        sub = lax.broadcasted_iota(jnp.int32, (16, TOK), 0)
        kst[b, E : E + 16, :] = jnp.where(sub == 0, f, 0.0).astype(jnp.bfloat16)
        return lax.dot_general(prob[i * NZ + o], kst[b], NT, preferred_element_type=jnp.float32)

    def sum_copy(o):
        back = (NZ - ring_order(o, NZ)) % NZ
        slot = ring_slot(back)
        return pltpu.make_async_remote_copy(
            src_ref=wsend.at[o], dst_ref=wrecv.at[slot],
            send_sem=sum_send.at[o], recv_sem=sum_recv.at[slot],
            device_id=at(dz=ring_order(o, NZ)), device_id_type=MESH,
        )

    def ring_slot(away):
        upper = away // (NZ // 2 + 1)
        odd = 2 * away - 1 + (1 - (away + NZ - 1) // NZ)
        return (1 - upper) * odd + upper * 2 * (NZ - away)

    def three(o, carry):
        acc[o] = weigh(0, o) + weigh(1, o) + weigh(2, o)
        return carry

    def finish(n, carry):
        o = NZ - 1 - n
        w = acc[o] + weigh(3, o)
        mass = w[:, E:].T[0:1, :]
        hi = mass.astype(jnp.bfloat16).astype(jnp.float32)
        lo = mass - hi
        rows = jnp.concatenate(
            [hi[:, :E], hi[:, E:], lo[:, :E], lo[:, E:], jnp.zeros((12, E), jnp.float32)], axis=0
        )
        wsend[o, :OWN, :] = w[:, :E].astype(jnp.bfloat16)
        wsend[o, OWN:, :] = rows.astype(jnp.bfloat16)

        @pl.when(o > 0)
        def _():
            sum_copy(o).start()

        return carry

    prepare(0)
    lax.fori_loop(0, 5, first, 0)
    for p in (1, 2):
        key_copy(p).wait_recv()
        core_copy(p).start()
    for p in (1, 2):
        core_copy(p).wait_recv()
    lax.fori_loop(0, 10, near, 0)
    key_copy(3).wait_recv()
    core_copy(3).start()
    lax.fori_loop(0, 9, far, 0)
    for i in range(3):
        send_stats(i)
    core_copy(3).wait_recv()
    lax.fori_loop(0, NZ, last, 0)
    send_stats(3)
    for i in range(3):
        finish_stats(i)
    lax.fori_loop(0, NZ, three, 0)
    finish_stats(3)
    lax.fori_loop(0, NZ, finish, 0)

    for o in range(1, NZ):
        sum_copy(o).wait_recv()
    total = wsend[0].astype(jnp.float32)
    for o in range(1, NZ):
        total = total + wrecv[o].astype(jnp.float32)
    mass = [total[OWN + h : OWN + h + 1] + total[OWN + 2 + h : OWN + 3 + h] for h in range(2)]
    for h in range(2):
        rows = slice(h * E, (h + 1) * E)
        down = jnp.broadcast_to(mass[h], (E, E)).T
        c = code[rows, :].astype(jnp.float32)
        new_code[rows, :] = ((total[rows] + c) / (down + 1.0)).astype(jnp.bfloat16)

    for p in range(1, NX):
        key_copy(p).wait_send()
        core_copy(p).wait_send()
    for o in range(1, NZ):
        code_copy(o).wait_send()
        sum_copy(o).wait_send()
    for i in range(NX):
        all_stats(i).wait_send()


def local(keys, code):
    vmem = pl.BlockSpec(memory_space=pltpu.VMEM)
    bf16, f32 = jnp.bfloat16, jnp.float32
    dma = pltpu.SemaphoreType.DMA
    new_code, loglik = pl.pallas_call(
        kernel,
        out_shape=(
            jax.ShapeDtypeStruct((OWN, E), bf16),
            jax.ShapeDtypeStruct((8, TOK // 8), f32),
        ),
        in_specs=[vmem, vmem],
        out_specs=(vmem, vmem),
        scratch_shapes=[
            pltpu.VMEM((NX, 2 * E, TOK), bf16),
            pltpu.VMEM((NZ, OWN, E), bf16),
            pltpu.VMEM((NZ, OWN, E), bf16),
            pltpu.VMEM((NX * NZ, OWN, TOK), bf16),
            pltpu.VMEM((NX, NZ, TOK), f32),
            pltpu.VMEM((NX, NZ, TOK), f32),
            pltpu.VMEM((NX, NZ, TOK), f32),
            pltpu.VMEM((2, 2 * E, TOK), bf16),
            pltpu.VMEM((NX, 32, 8, TOK // 8), f32),
            pltpu.VMEM((NZ, OWN, 2 * E), f32),
            pltpu.VMEM((NZ, OWN + 16, E), bf16),
            pltpu.VMEM((NZ, OWN + 16, E), bf16),
            dma((NX,)), dma((NX,)), dma((NX,)), dma((NX,)),
            dma((NZ,)), dma((NZ,)), dma((NX,)), dma((NX,)),
            dma((NZ,)), dma((NZ,)),
        ],
        compiler_params=pltpu.CompilerParams(
            collective_id=0, has_side_effects=True, vmem_limit_bytes=48 * 2**20
        ),
    )(keys, code)
    return new_code, loglik.reshape(TOK)


def solution(mesh):
    return jax.shard_map(
        local,
        mesh=mesh,
        in_specs=(P("dp", None), P(("dp", "codebook"), None)),
        out_specs=(P(("dp", "codebook"), None), P("dp")),
        check_vma=False,
    )
```

time: 364 us -> 69.6 us (0.19)
  blocking collectives: 142 us -> 0 us
  waiting for transfers between devices: 124 us -> 0 us
  Pallas kernels: 0 us -> 65.8 us
  matrix products: 46.9 us -> 0 us
  other arithmetic: 31.1 us -> 0 us
  between operations: 14.1 us -> 0.65 us
    psum x2 -> x0, blocking collectives: 125 us -> none  [the longest x1 113 us: local(): weighted, mass = lax.psum((weighted, mass), 'dp')]
    all_gather x1 -> x0, waiting for transfers between devices: 79.3 us -> none  [local(): local_entries = lax.all_gather(codebook, 'dp', axis=0, tiled=True)]
    pallas_call x0 -> x1, Pallas kernels: none -> 65.8 us  [local(): pl.pallas_call(kernel, out_shape=(jax.ShapeDtypeStruct((OWN, E), bf16), j...]
    dot_general x24 -> x0, matrix products: 46.9 us -> none  [the longest x16 34.5 us: scores_of(): cross = jnp.dot(keys, block.T, preferred_element_type=jnp.float32)]
    psum x1 -> x0, waiting for transfers between devices: 44 us -> none  [local(): weighted, mass = lax.psum((weighted, mass), 'dp')]
    reduce_sum x26 -> x0, other arithmetic: 29.3 us -> none  [the longest x16 18.9 us: scores_of(): sq_code = jnp.sum(block_f * block_f, axis=1)]
    pmax x1 -> x0, blocking collectives: 16.3 us -> none  [local(): peak = lax.pmax(peak_local, 'codebook')]
  transfers between devices with their start and end apart: 2 -> 0, of which waited for: 2 -> 0; matrix products, arithmetic and copies ran while one was open for 0% -> 0% of each run, Pallas kernels for 0% -> 0%
where the time goes in v1:
time: 69.6 us; the launch traced here: 69.5 us
  Pallas kernels  65.8 us (95%)
  local copies, waits for them, and re-layouts  3.01 us (4%)
    pallas_call x1, Pallas kernels, local(): pl.pallas_call(kernel, out_shape=(jax.ShapeDtypeStruct((OWN, E), bf16), j...  65.8 us
    unnamed x6, local copies, waits for them, and re-layouts  3.01 us

profile of v1, /device:TPU:1, one launch (start us, length us, event | category | flops | bytes accessed | tf_op | source)
XLA Modules:
  0.0 69.5 jit_solution(2911122185317962690)
XLA Ops:
  0.6 0.0 copy-start
  0.6 0.9 %copy-done = bf16[1024,128]{1,0:T(8,128)(2,1)S(1)} copy-done((bf16[1024,128]{1,0:T(8,128)(2,1)S(1)}, bf16[1024,128]{1,0:T(8,128)(2,1)}, u32[]{:S(2)}) %copy-start) | copy-done | bytes 262168
  1.6 0.0 copy-start.1
  1.6 0.8 %copy-done.1 = bf16[256,128]{1,0:T(8,128)(2,1)S(1)} copy-done((bf16[256,128]{1,0:T(8,128)(2,1)S(1)}, bf16[256,128]{1,0:T(8,128)(2,1)}, u32[]{:S(2)}) %copy-start.1) | copy-done | bytes 65560
  2.4 65.8 %shard_map.41 = (bf16[256,128]{1,0:T(8,128)(2,1)S(1)}, f32[8,128]{1,0:T(8,128)S(1)}) custom-call(bf16[1024,128]{1,0:T(8,128)(2,1)S(1)} %copy-done, bf16[256,128]{1,0:T(8,128)(2,1)S(1)} %copy-done.1), custom_call_target="tpu_custom_call" | custom-call | tf_op jit(solution)/shard_map/pallas_call | solution.py:295
  68.3 0.6 copy.6
  68.9 0.6 copy.7
Async XLA Ops:
  0.6 1.0 %copy-start = (bf16[1024,128]{1,0:T(8,128)(2,1)S(1)}, bf16[1024,128]{1,0:T(8,128)(2,1)}, u32[]{:S(2)}) copy-start(bf16[1024,128]{1,0:T(8,128)(2,1)} %keys.1) | copy-start | bytes 786436
  1.6 0.8 %copy-start.1 = (bf16[256,128]{1,0:T(8,128)(2,1)S(1)}, bf16[256,128]{1,0:T(8,128)(2,1)}, u32[]{:S(2)}) copy-start(bf16[256,128]{1,0:T(8,128)(2,1)} %code.1) | copy-start | bytes 196612

commit v2 on v0

v2 whole, which is shorter than its diff:
```python
import jax
import jax.numpy as jnp
from jax import lax
from jax.experimental import pallas as pl
from jax.experimental.pallas import tpu as pltpu
from jax.sharding import PartitionSpec as P

MESH = pl.DeviceIdType.MESH
NX, NZ, NY = 4, 8, 4
TOK, OWN, E = 1024, 256, 128
TILE = 256
HALF = OWN // 2 + 16
BETA = 0.1
LOG2E = 1.4426950408889634
LN2 = 0.6931471805599453
ALPHA = 2.0 * BETA * LOG2E
NT = (((1,), (1,)), ((), ()))
KEY_AT = (0, 1, 3, 2)
KEY_SLOT = (0, 1, 3, 2)
CODE_AT = (0, 1, 7, 2, 6, 3, 5, 4)


def to_tile(row):
    return jnp.concatenate([row[:, 128 * r : 128 * (r + 1)] for r in range(8)], axis=0)


def to_row(tile):
    return jnp.concatenate([tile[r : r + 1, :] for r in range(8)], axis=1)


def kernel(
    keys, code, new_code, loglik,
    raw, kt, cb, prob, top, tot, scale, s0, s1, x0, x1, stats, acc, wsend, wnear, wfar, wrecv,
    in_sem, key_send, key_recv, core_send, core_recv, code_send, code_recv,
    stat_send, stat_recv, sum_send, sum_recv,
):
    dp, col = lax.axis_index("dp"), lax.axis_index("codebook")
    x, z = dp >> 3, dp & 7
    y, core = col >> 1, col & 1
    xs = [((x + d) & 3) << 3 for d in range(NX)]
    zs = [(z + d) & 7 for d in range(NZ)]
    cols = [[(((y + d) & 3) << 1) + ((core + c) & 1) for c in range(2)] for d in range(NY)]

    def at(dx=0, dz=0, dy=0, dc=0):
        return (xs[dx % NX] + zs[dz % NZ], cols[dy % NY][dc % 2])

    others = [(dx, dy, dc) for dx in range(4) for dy in range(4) for dc in range(2)][1:]

    barrier = pltpu.get_barrier_semaphore()
    for dz in range(1, NZ):
        pl.semaphore_signal(barrier, inc=1, device_id=at(dz=dz), device_id_type=MESH)
    for dx, dy, dc in others:
        pl.semaphore_signal(
            barrier, inc=1, device_id=at(dx=dx, dy=dy, dc=dc), device_id_type=MESH
        )

    get_code = pltpu.make_async_copy(code, cb.at[0, :, :E], in_sem.at[0])
    get_keys = pltpu.make_async_copy(keys, raw, in_sem.at[1])
    get_keys.start()
    get_code.start()
    row = lax.broadcasted_iota(jnp.int32, (E, TOK), 0)
    ones = jnp.where(row < 3, 1.0, 0.0).astype(jnp.bfloat16)
    for i in range(NX):
        kt[i, E:, :] = ones
    get_keys.wait()
    kt[0, :E, :] = raw[...].astype(jnp.float32).T.astype(jnp.bfloat16)
    get_code.wait()

    half = pl.ds(pl.multiple_of(core * (E // 2), E // 2), E // 2)

    def remote(src, dst, send, recv, to):
        return pltpu.make_async_remote_copy(
            src_ref=src, dst_ref=dst, send_sem=send, recv_sem=recv,
            device_id=to, device_id_type=MESH,
        )

    def key_copy(p):
        return remote(
            kt.at[0, half], kt.at[p, half], key_send.at[p], key_recv.at[p], at(dx=-KEY_AT[p])
        )

    def core_copy(p):
        return remote(
            kt.at[p, half], kt.at[p, half], core_send.at[p], core_recv.at[p], at(dc=1)
        )

    def code_copy(o):
        return remote(
            cb.at[0, :, :E], cb.at[o, :, :E], code_send.at[o], code_recv.at[o], at(dz=-CODE_AT[o])
        )

    def pass_on(o):
        src, dst, dz = ((3, 5, -1), (4, 6, 1), (3, 7, -2), (4, 7, 2))[o - 5]
        rows = (slice(None), slice(None), slice(0, OWN // 2), slice(OWN // 2, OWN))[o - 5]
        return remote(
            cb.at[src, rows, :E], cb.at[dst, rows, :E], code_send.at[o], code_recv.at[o], at(dz=dz)
        )

    def prepare(o):
        c = cb[o, :, :E].astype(jnp.float32)
        h = -0.5 * jnp.sum(c * c, axis=1, keepdims=True)
        hi = h.astype(jnp.bfloat16).astype(jnp.float32)
        mid = (h - hi).astype(jnp.bfloat16).astype(jnp.float32)
        lo = h - hi - mid
        lane = lax.broadcasted_iota(jnp.int32, (OWN, E), 1)
        both = jnp.where(lane == 0, hi, jnp.where(lane == 1, mid, lo))
        cb[o, :, E:] = jnp.where(lane < 3, both, 0.0).astype(jnp.bfloat16)

    prepare(0)
    pl.semaphore_wait(barrier, len(others) + NZ - 1)
    for p in (1, 2):
        key_copy(p).start()
    for o in (3, 4, 1, 2):
        code_copy(o).start()

    def place(u):
        a = (u + 27) // 32
        b = (u + 22) // 32
        c = (u + 17) // 32
        d = (u + 8) // 32
        near_i = a + b
        near_o = u - 5 * near_i
        t = u - 15
        far_i = t - 3 * (t // 3)
        far_o = 5 + t // 3
        i = (1 - c) * near_i + (c - d) * far_i + 3 * d
        o = (1 - c) * near_o + (c - d) * far_o + d * (u - 24)
        return i, o

    def cross(u, s, m):
        i, o = place(u)
        for q in range(TOK // TILE):
            span = slice(q * TILE, (q + 1) * TILE)
            v = jnp.dot(cb[o], kt[i, :, span], preferred_element_type=jnp.float32)
            s[:, span] = v
            m[:, span] = jnp.max(v.reshape(OWN // 8, 8, TILE), axis=0)
            yield

    def power(u, s, m):
        i, o = place(u)
        k = i * NZ + o
        for q in range(TOK // TILE):
            span = slice(q * TILE, (q + 1) * TILE)
            peak = jnp.max(m[:, span], axis=0, keepdims=True)
            p = jnp.exp2((s[:, span] - peak) * ALPHA)
            top[k, :, span] = jnp.broadcast_to(peak, (8, TILE))
            tot[k, :, span] = jnp.sum(p.reshape(OWN // 8, 8, TILE), axis=0)
            prob[k, :, span] = p.astype(jnp.bfloat16)
            yield

    def both(u, later, now):
        for _ in zip(cross(u + 1, *later), power(u, *now)):
            pass

    def stat_copy(i, r):
        dx, dy, dc = others[r - 1]
        slot = KEY_SLOT[(KEY_AT[i] - dx) % NX]
        return remote(
            stats.at[i, 0], stats.at[slot, r], stat_send.at[i], stat_recv.at[slot],
            at(dx=dx, dy=dy, dc=dc),
        )

    def all_stats(i):
        return remote(
            stats.at[i, pl.ds(1, 31)], stats.at[i, pl.ds(1, 31)],
            stat_send.at[i], stat_recv.at[i], at(dc=1),
        )

    def send_stats(i):
        m = [top[i * NZ + o] for o in range(NZ)]
        peak = m[0]
        for o in range(1, NZ):
            peak = jnp.maximum(peak, m[o])
        total = jnp.zeros_like(peak)
        for o in range(NZ):
            total = total + tot[i * NZ + o] * jnp.exp2((m[o] - peak) * ALPHA)
        total = jnp.sum(total, axis=0, keepdims=True)
        stats[i, 0] = to_tile(ALPHA * peak[0:1] + jnp.log2(total))
        for r in range(1, 32):
            stat_copy(i, r).start()

    def finish_stats(i):
        all_stats(i).wait_recv()
        v = stats[i]
        peak = jnp.max(v, axis=0)
        lse = peak + jnp.log2(jnp.sum(jnp.exp2(v - peak[None]), axis=0))
        if i == 0:
            k = kt[0, :E, :].astype(jnp.float32)
            sq = to_tile(jnp.sum(k * k, axis=0, keepdims=True))
            loglik[...] = LN2 * lse - BETA * sq
        lse = jnp.broadcast_to(to_row(lse), (8, TOK))
        for o in range(NZ):
            f = jnp.exp2(ALPHA * top[i * NZ + o] - lse)
            scale[i * NZ + o] = jnp.concatenate([f, f], axis=0).astype(jnp.bfloat16)

    def on(u, k):
        return pl.when(u == k)

    def ready(u):
        for o in (1, 2, 3, 4):

            @on(u, o)
            def _():
                code_copy(o).wait_recv()
                if o == 3:
                    pass_on(5).start()
                    pass_on(7).start()
                if o == 4:
                    pass_on(6).start()
                    pass_on(8).start()
                prepare(o)

        @on(u, 5)
        def _():
            for p in (1, 2):
                key_copy(p).wait_recv()
                core_copy(p).start()
            key_copy(3).start()
            core_copy(1).wait_recv()

        @on(u, 10)
        def _():
            core_copy(2).wait_recv()

        for o in (5, 6, 7):

            @on(u, 15 + 3 * (o - 5))
            def _():
                if o == 5:
                    key_copy(3).wait_recv()
                    core_copy(3).start()
                pass_on(o).wait_recv()
                if o == 7:
                    pass_on(8).wait_recv()
                prepare(o)

        @on(u, 24)
        def _():
            core_copy(3).wait_recv()

        @on(u, 25)
        def _():
            for i in range(3):
                send_stats(i)

    a, b = (s0, x0), (s1, x1)
    for _ in cross(0, *a):
        pass

    def two(n, carry):
        ready(2 * n + 1)
        both(2 * n, b, a)
        ready(2 * n + 2)
        both(2 * n + 1, a, b)
        return carry

    lax.fori_loop(0, 15, two, 0)
    both(30, b, a)
    for _ in power(31, *b):
        pass
    send_stats(3)

    def weigh(i, o):
        k = i * NZ + o
        p = prob[k].reshape(OWN // 16, 16, TOK) * scale[k][None]
        return lax.dot_general(p.reshape(OWN, TOK), kt[i], NT, preferred_element_type=jnp.float32)

    def three(o, carry):
        acc[o] = weigh(0, o) + weigh(1, o) + weigh(2, o)
        return carry

    for i in range(3):
        finish_stats(i)
    lax.fori_loop(0, NZ, three, 0)
    finish_stats(3)

    def far_copy(o):
        src, dst, dz = (
            (wsend.at[5], wnear.at[0], 1),
            (wsend.at[6], wnear.at[1], -1),
            (wsend.at[7, 0], wfar.at[0], 2),
            (wsend.at[7, 1], wfar.at[1], -2),
        )[o - 5]
        return remote(src, dst, sum_send.at[o], sum_recv.at[o], at(dz=dz))

    def near_copy(o):
        return remote(
            wsend.at[o], wrecv.at[o], sum_send.at[o], sum_recv.at[o], at(dz=CODE_AT[o])
        )

    def finish(n, carry):
        o = NZ - 1 - n
        w = acc[o] + weigh(3, o)
        mass = w[:, E:].T[0:1, :]
        hi = mass.astype(jnp.bfloat16).astype(jnp.float32)
        lo = mass - hi
        for h in range(2):
            rows = slice(h * E, (h + 1) * E)
            wsend[o, h, :E, :] = w[rows, :E].astype(jnp.bfloat16)
            wsend[o, h, E:, :] = jnp.concatenate(
                [hi[:, rows], lo[:, rows], jnp.zeros((14, E), jnp.float32)], axis=0
            ).astype(jnp.bfloat16)

        @on(o, 7)
        def _():
            far_copy(7).start()
            far_copy(8).start()

        for k in (5, 6):

            @on(o, k)
            def _():
                far_copy(k).start()

        for k in (1, 2):

            @on(o, k)
            def _():
                near_copy(k).start()

        return carry

    lax.fori_loop(0, NZ, finish, 0)

    for r in range(2):
        far_copy(5 + r).wait_recv()
        far_copy(7 + r).wait_recv()
        for h in range(2):
            total = wsend[3 + r, h].astype(jnp.float32) + wnear[r, h].astype(jnp.float32)
            if h == r:
                total = total + wfar[r].astype(jnp.float32)
            mass = total[E : E + 1] + total[E + 1 : E + 2]
            hi = mass.astype(jnp.bfloat16).astype(jnp.float32)
            wsend[3 + r, h, :E, :] = total[:E].astype(jnp.bfloat16)
            wsend[3 + r, h, E:, :] = jnp.concatenate(
                [hi, mass - hi, jnp.zeros((14, E), jnp.float32)], axis=0
            ).astype(jnp.bfloat16)
        near_copy(3 + r).start()

    for o in (1, 2, 3, 4):
        near_copy(o).wait_recv()
    for h in range(2):
        total = wsend[0, h].astype(jnp.float32)
        for o in (1, 2, 3, 4):
            total = total + wrecv[o, h].astype(jnp.float32)
        mass = jnp.broadcast_to(total[E : E + 1] + total[E + 1 : E + 2], (E, E)).T
        rows = slice(h * E, (h + 1) * E)
        c = cb[0, rows, :E].astype(jnp.float32)
        new_code[rows, :] = ((total[:E] + c) / (mass + 1.0)).astype(jnp.bfloat16)

    for p in (1, 2, 3):
        key_copy(p).wait_send()
        core_copy(p).wait_send()
    for o in (1, 2, 3, 4):
        code_copy(o).wait_send()
        near_copy(o).wait_send()
    for o in (5, 6, 7, 8):
        pass_on(o).wait_send()
        far_copy(o).wait_send()
    for i in range(NX):
        all_stats(i).wait_send()


def local(keys, code):
    vmem = pl.BlockSpec(memory_space=pltpu.VMEM)
    hbm = pl.BlockSpec(memory_space=pl.ANY)
    bf16, f32 = jnp.bfloat16, jnp.float32
    dma = pltpu.SemaphoreType.DMA
    new_code, loglik = pl.pallas_call(
        kernel,
        out_shape=(
            jax.ShapeDtypeStruct((OWN, E), bf16),
            jax.ShapeDtypeStruct((8, TOK // 8), f32),
        ),
        in_specs=[hbm, hbm],
        out_specs=(vmem, vmem),
        scratch_shapes=[
            pltpu.VMEM((TOK, E), bf16),
            pltpu.VMEM((NX, 2 * E, TOK), bf16),
            pltpu.VMEM((NZ, OWN, 2 * E), bf16),
            pltpu.VMEM((NX * NZ, OWN, TOK), bf16),
            pltpu.VMEM((NX * NZ, 8, TOK), f32),
            pltpu.VMEM((NX * NZ, 8, TOK), f32),
            pltpu.VMEM((NX * NZ, 16, TOK), bf16),
            pltpu.VMEM((OWN, TOK), f32),
            pltpu.VMEM((OWN, TOK), f32),
            pltpu.VMEM((8, TOK), f32),
            pltpu.VMEM((8, TOK), f32),
            pltpu.VMEM((NX, 32, 8, TOK // 8), f32),
            pltpu.VMEM((NZ, OWN, 2 * E), f32),
            pltpu.VMEM((NZ, 2, HALF, E), bf16),
            pltpu.VMEM((2, 2, HALF, E), bf16),
            pltpu.VMEM((2, HALF, E), bf16),
            pltpu.VMEM((5, 2, HALF, E), bf16),
            dma((2,)),
            dma((NX,)), dma((NX,)), dma((NX,)), dma((NX,)),
            dma((NZ + 1,)), dma((NZ + 1,)),
            dma((NX,)), dma((NX,)), dma((NZ + 1,)), dma((NZ + 1,)),
        ],
        compiler_params=pltpu.CompilerParams(
            collective_id=0, has_side_effects=True, vmem_limit_bytes=48 * 2**20
        ),
    )(keys, code)
    return new_code, loglik.reshape(TOK)


def solution(mesh):
    return jax.shard_map(
        local,
        mesh=mesh,
        in_specs=(P("dp", None), P(("dp", "codebook"), None)),
        out_specs=(P(("dp", "codebook"), None), P("dp")),
        check_vma=False,
    )
```

time: 364 us -> 59.7 us (0.16)
  blocking collectives: 142 us -> 0 us
  waiting for transfers between devices: 124 us -> 0 us
  Pallas kernels: 0 us -> 55.9 us
  matrix products: 46.9 us -> 0 us
  other arithmetic: 31.1 us -> 0 us
  between operations: 14.1 us -> 0.65 us
    psum x2 -> x0, blocking collectives: 125 us -> none  [the longest x1 113 us: local(): weighted, mass = lax.psum((weighted, mass), 'dp')]
    all_gather x1 -> x0, waiting for transfers between devices: 79.3 us -> none  [local(): local_entries = lax.all_gather(codebook, 'dp', axis=0, tiled=True)]
    pallas_call x0 -> x1, Pallas kernels: none -> 55.9 us  [local(): pl.pallas_call(kernel, out_shape=(jax.ShapeDtypeStruct((OWN, E), bf16), j...]
    dot_general x24 -> x0, matrix products: 46.9 us -> none  [the longest x16 34.5 us: scores_of(): cross = jnp.dot(keys, block.T, preferred_element_type=jnp.float32)]
    psum x1 -> x0, waiting for transfers between devices: 44 us -> none  [local(): weighted, mass = lax.psum((weighted, mass), 'dp')]
    reduce_sum x26 -> x0, other arithmetic: 29.3 us -> none  [the longest x16 18.9 us: scores_of(): sq_code = jnp.sum(block_f * block_f, axis=1)]
    pmax x1 -> x0, blocking collectives: 16.3 us -> none  [local(): peak = lax.pmax(peak_local, 'codebook')]
  transfers between devices with their start and end apart: 2 -> 0, of which waited for: 2 -> 0; matrix products, arithmetic and copies ran while one was open for 0% -> 0% of each run, Pallas kernels for 0% -> 0%
where the time goes in v2:
time: 59.7 us; the launch traced here: 59.6 us
  Pallas kernels  55.9 us (94%)
  local copies, waits for them, and re-layouts  3.01 us (5%)
  between operations  0.65 us (1%)
    pallas_call x1, Pallas kernels, local(): pl.pallas_call(kernel, out_shape=(jax.ShapeDtypeStruct((OWN, E), bf16), j...  55.9 us
    unnamed x6, local copies, waits for them, and re-layouts  3.01 us

profile of v2, /device:TPU:1, one launch (start us, length us, event | category | flops | bytes accessed | tf_op | source)
XLA Modules:
  0.0 59.6 jit_solution(7017860690835327985)
XLA Ops:
  0.6 0.0 copy-start
  0.6 0.9 %copy-done = bf16[1024,128]{1,0:T(8,128)(2,1)S(1)} copy-done((bf16[1024,128]{1,0:T(8,128)(2,1)S(1)}, bf16[1024,128]{1,0:T(8,128)(2,1)}, u32[]{:S(2)}) %copy-start) | copy-done | bytes 262168
  1.6 0.0 copy-start.1
  1.6 0.8 %copy-done.1 = bf16[256,128]{1,0:T(8,128)(2,1)S(1)} copy-done((bf16[256,128]{1,0:T(8,128)(2,1)S(1)}, bf16[256,128]{1,0:T(8,128)(2,1)}, u32[]{:S(2)}) %copy-start.1) | copy-done | bytes 65560
  2.4 55.9 %shard_map.41 = (bf16[256,128]{1,0:T(8,128)(2,1)S(1)}, f32[8,128]{1,0:T(8,128)S(1)}) custom-call(bf16[1024,128]{1,0:T(8,128)(2,1)S(1)} %copy-done, bf16[256,128]{1,0:T(8,128)(2,1)S(1)} %copy-done.1), custom_call_target="tpu_custom_call" | custom-call | tf_op jit(solution)/shard_map/pallas_call | solution.py:369
  58.4 0.6 %copy.6 = bf16[256,128]{1,0:T(8,128)(2,1)} copy(bf16[256,128]{1,0:T(8,128)(2,1)S(1)} %get-tuple-element.8) | data formatting | bytes 131072
  59.0 0.6 copy.7
Async XLA Ops:
  0.6 1.0 %copy-start = (bf16[1024,128]{1,0:T(8,128)(2,1)S(1)}, bf16[1024,128]{1,0:T(8,128)(2,1)}, u32[]{:S(2)}) copy-start(bf16[1024,128]{1,0:T(8,128)(2,1)} %keys.1) | copy-start | bytes 786436
  1.6 0.8 %copy-start.1 = (bf16[256,128]{1,0:T(8,128)(2,1)S(1)}, bf16[256,128]{1,0:T(8,128)(2,1)}, u32[]{:S(2)}) copy-start(bf16[256,128]{1,0:T(8,128)(2,1)} %code.1) | copy-start | bytes 196612

commit v3 on v2

v3 whole, which is shorter than its diff:
```python
import jax
import jax.numpy as jnp
from jax import lax
from jax.experimental import pallas as pl
from jax.experimental.pallas import tpu as pltpu
from jax.sharding import PartitionSpec as P

MESH = pl.DeviceIdType.MESH
NX, NZ, NY = 4, 8, 4
TOK, OWN, E = 1024, 256, 128
TILE = 256
HALF = OWN // 2 + 16
BETA = 0.1
LOG2E = 1.4426950408889634
LN2 = 0.6931471805599453
ALPHA = 2.0 * BETA * LOG2E
NT = (((1,), (1,)), ((), ()))
CODE_AT = (0, 2, 6, 1, 7, 3, 5, 4)


def to_tile(row):
    return jnp.concatenate([row[:, 128 * r : 128 * (r + 1)] for r in range(8)], axis=0)


def to_row(tile):
    return jnp.concatenate([tile[r : r + 1, :] for r in range(8)], axis=1)


def kernel(
    keys, code, new_code, loglik,
    raw, kt, cb, prob, top, tot, scale, s0, s1, x0, x1, stats, mine, acc, wsend, wnear, wfar, wrecv,
    in_sem, key_send, key_recv, core_send, core_recv, code_send, code_recv,
    stat_send, stat_recv, sum_send, sum_recv,
):
    dp, col = lax.axis_index("dp"), lax.axis_index("codebook")
    x, z = dp >> 3, dp & 7
    y, core = col >> 1, col & 1
    xs = [((x + d) & 3) << 3 for d in range(NX)]
    zs = [(z + d) & 7 for d in range(NZ)]
    cols = [[(((y + d) & 3) << 1) + ((core + c) & 1) for c in range(2)] for d in range(NY)]

    def at(dx=0, dz=0, dy=0, dc=0):
        return (xs[dx % NX] + zs[dz % NZ], cols[dy % NY][dc % 2])

    others = [(dx, dy, dc) for dx in range(4) for dy in range(4) for dc in range(2)][1:]

    barrier = pltpu.get_barrier_semaphore()
    for dz in range(1, NZ):
        pl.semaphore_signal(barrier, inc=1, device_id=at(dz=dz), device_id_type=MESH)
    for dx, dy, dc in others:
        pl.semaphore_signal(
            barrier, inc=1, device_id=at(dx=dx, dy=dy, dc=dc), device_id_type=MESH
        )

    get_code = pltpu.make_async_copy(code, cb.at[0, :, :E], in_sem.at[0])
    get_keys = pltpu.make_async_copy(keys, raw, in_sem.at[1])
    get_keys.start()
    get_code.start()
    row = lax.broadcasted_iota(jnp.int32, (E, TOK), 0)
    ones = jnp.where(row < 3, 1.0, 0.0).astype(jnp.bfloat16)
    for i in range(NX):
        kt[i, E:, :] = ones
    acc[...] = jnp.zeros_like(acc)
    get_keys.wait()
    kt[0, :E, :] = raw[...].astype(jnp.float32).T.astype(jnp.bfloat16)
    get_code.wait()

    def quarter(h):
        return pl.ds(pl.multiple_of(core * (E // 2) + h * (E // 4), E // 4), E // 4)

    half = pl.ds(pl.multiple_of(core * (E // 2), E // 2), E // 2)

    def remote(src, dst, send, recv, to):
        return pltpu.make_async_remote_copy(
            src_ref=src, dst_ref=dst, send_sem=send, recv_sem=recv,
            device_id=to, device_id_type=MESH,
        )

    def key_copy(p, h):
        src = p if p < 3 else 2 - h
        dx = {1: -1, 2: 1}[src]
        return remote(
            kt.at[0 if p < 3 else src, quarter(h)], kt.at[p, quarter(h)],
            key_send.at[2 * p + h], key_recv.at[2 * p + h], at(dx=dx),
        )

    def core_copy(p):
        return remote(
            kt.at[p, half], kt.at[p, half], core_send.at[p], core_recv.at[p], at(dc=1)
        )

    def code_copy(o):
        return remote(
            cb.at[0, :, :E], cb.at[o, :, :E], code_send.at[o], code_recv.at[o], at(dz=-CODE_AT[o])
        )

    def pass_on(o):
        src, dst, dz = ((1, 5, -1), (2, 6, 1), (1, 7, -2), (2, 7, 2))[o - 5]
        rows = (slice(None), slice(None), slice(0, OWN // 2), slice(OWN // 2, OWN))[o - 5]
        return remote(
            cb.at[src, rows, :E], cb.at[dst, rows, :E], code_send.at[o], code_recv.at[o], at(dz=dz)
        )

    def prepare(o):
        c = cb[o, :, :E].astype(jnp.float32)
        h = -0.5 * jnp.sum(c * c, axis=1, keepdims=True)
        hi = h.astype(jnp.bfloat16).astype(jnp.float32)
        mid = (h - hi).astype(jnp.bfloat16).astype(jnp.float32)
        lo = h - hi - mid
        lane = lax.broadcasted_iota(jnp.int32, (OWN, E), 1)
        both = jnp.where(lane == 0, hi, jnp.where(lane == 1, mid, lo))
        cb[o, :, E:] = jnp.where(lane < 3, both, 0.0).astype(jnp.bfloat16)

    prepare(0)
    pl.semaphore_wait(barrier, len(others) + NZ - 1)
    for p, h in ((1, 1), (2, 0), (1, 0), (2, 1)):
        key_copy(p, h).start()
    for o in (1, 2, 3, 4):
        code_copy(o).start()

    def place(u):
        near_i = (u + 27) // 32 + (u + 22) // 32
        near_o = u - 5 * near_i
        far = (u + 17) // 32
        t = u - 15
        opposite = (x + 2) & 3
        t1 = t - 3 * opposite
        t2 = t1 - 8
        b = (t1 + 32) // 32
        c = (t2 + 32) // 32
        n1, n2 = t // 3, t2 // 3
        owner = (1 - b) * n1 + (b - c) * opposite + c * (opposite + 1 + n2)
        away = (owner - x) & 3
        far_i = away + (away >> 1) - 2 * ((away + 1) >> 2)
        far_o = (1 - b) * (5 + t - 3 * n1) + (b - c) * t1 + c * (5 + t2 - 3 * n2)
        return (1 - far) * near_i + far * far_i, (1 - far) * near_o + far * far_o

    def cross(u, s, m):
        i, o = place(u)
        for q in range(TOK // TILE):
            span = slice(q * TILE, (q + 1) * TILE)
            v = jnp.dot(cb[o], kt[i, :, span], preferred_element_type=jnp.float32)
            s[:, span] = v
            m[:, span] = jnp.max(v.reshape(OWN // 8, 8, TILE), axis=0)
            yield

    def power(u, s, m):
        i, o = place(u)
        k = i * NZ + o
        for q in range(TOK // TILE):
            span = slice(q * TILE, (q + 1) * TILE)
            peak = jnp.max(m[:, span], axis=0, keepdims=True)
            p = jnp.exp2((s[:, span] - peak) * ALPHA)
            top[k, :, span] = jnp.broadcast_to(peak, (8, TILE))
            tot[k, :, span] = jnp.sum(p.reshape(OWN // 8, 8, TILE), axis=0)
            prob[k, :, span] = p.astype(jnp.bfloat16)
            yield

    def both(u, later, now):
        for _ in zip(cross(u + 1, *later), power(u, *now)):
            pass

    def all_stats(owner):
        return remote(
            stats.at[owner, pl.ds(1, 31)], stats.at[owner, pl.ds(1, 31)],
            stat_send.at[owner], stat_recv.at[owner], at(dc=1),
        )

    def slot_of(owner):
        away = (owner - x) & 3
        return away + (away >> 1) - 2 * ((away + 1) >> 2)

    def send_stats(owner):
        first = slot_of(owner) * NZ
        m = [top[first + o] for o in range(NZ)]
        peak = m[0]
        for o in range(1, NZ):
            peak = jnp.maximum(peak, m[o])
        total = jnp.zeros_like(peak)
        for o in range(NZ):
            total = total + tot[first + o] * jnp.exp2((m[o] - peak) * ALPHA)
        total = jnp.sum(total, axis=0, keepdims=True)
        stats[owner, 0] = to_tile(ALPHA * peak[0:1] + jnp.log2(total))
        for r, (dx, dy, dc) in enumerate(others):
            remote(
                stats.at[owner, 0], stats.at[owner, r + 1],
                stat_send.at[owner], stat_recv.at[owner], at(dx=dx, dy=dy, dc=dc),
            ).start()

    def finish_stats(owner):
        all_stats(owner).wait_recv()
        first = slot_of(owner) * NZ
        v = stats[owner]
        peak = jnp.max(v, axis=0)
        lse = peak + jnp.log2(jnp.sum(jnp.exp2(v - peak[None]), axis=0))
        mine[owner] = lse
        lse = jnp.broadcast_to(to_row(lse), (8, TOK))
        for o in range(NZ):
            f = jnp.exp2(ALPHA * top[first + o] - lse)
            scale[first + o] = jnp.concatenate([f, f], axis=0).astype(jnp.bfloat16)

    def on(u, k):
        return pl.when(u == k)

    def need_code(o):
        if o < 5:
            code_copy(o).wait_recv()
            if o < 3:
                pass_on(4 + o).start()
                pass_on(6 + o).start()
        else:
            pass_on(o).wait_recv()
        if o == 7:
            pass_on(8).wait_recv()
        prepare(o)

    turn = ((s0, x0), (s1, x1))

    def steps(u, n):
        for j in range(n):
            both(u + j, turn[(j + 1) % 2], turn[j % 2])

    for _ in cross(0, *turn[0]):
        pass
    need_code(1)
    need_code(2)
    for p, h in ((1, 1), (2, 0)):
        key_copy(p, h).wait_recv()
        key_copy(3, h).start()
    for p, h in ((1, 0), (2, 1)):
        key_copy(p, h).wait_recv()
        core_copy(p).start()
    need_code(3)
    need_code(4)

    def near(n, carry):
        for p in (1, 2):
            on(n, p)(lambda p=p: core_copy(p).wait_recv())
        steps(4 * n, 4)
        return carry

    lax.fori_loop(0, 3, near, 0)
    key_copy(3, 0).wait_recv()
    key_copy(3, 1).wait_recv()
    core_copy(3).start()
    steps(12, 2)
    for o in (5, 6, 7):
        need_code(o)
    core_copy(3).wait_recv()

    def done(owner):
        opposite = (x + 2) & 3
        return 17 + 3 * owner + 5 * ((owner - opposite + 4) >> 2)

    def far(n, carry):
        u = 14 + 4 * n
        steps(u, 4)
        for owner in range(3):
            when = (done(owner) - 14) >> 2
            on(n, when)(lambda owner=owner: send_stats(owner))
        return carry

    lax.fori_loop(0, 4, far, 0)
    both(30, turn[1], turn[0])
    for _ in power(31, *turn[1]):
        pass
    send_stats(3)

    def weigh(owner, o, m):
        i = slot_of(owner)
        span = pl.ds(i * NZ + o, m)
        p = prob[span].reshape(m, OWN // 16, 16, TOK) * scale[span][:, None]
        p = p.reshape(m * OWN, TOK)
        w = lax.dot_general(p, kt[i], NT, preferred_element_type=jnp.float32)
        acc[pl.ds(o, m)] += w.reshape(m, OWN, 2 * E)

    def shard(owner, carry):
        finish_stats(owner)
        weigh(owner, 0, NZ)
        return carry

    lax.fori_loop(0, 3, shard, 0)
    finish_stats(3)

    def far_copy(o):
        src, dst, dz = (
            (wsend.at[5], wnear.at[0], 1),
            (wsend.at[6], wnear.at[1], -1),
            (wsend.at[7, 0], wfar.at[0], 2),
            (wsend.at[7, 1], wfar.at[1], -2),
        )[o - 5]
        return remote(src, dst, sum_send.at[o], sum_recv.at[o], at(dz=dz))

    def near_copy(o):
        return remote(
            wsend.at[o], wrecv.at[o], sum_send.at[o], sum_recv.at[o], at(dz=CODE_AT[o])
        )

    def pack(o):
        w = acc[o]
        mass = w[:, E:].T[0:1, :]
        hi = mass.astype(jnp.bfloat16).astype(jnp.float32)
        lo = mass - hi
        for h in range(2):
            rows = slice(h * E, (h + 1) * E)
            wsend[o, h, :E, :] = w[rows, :E].astype(jnp.bfloat16)
            wsend[o, h, E:, :] = jnp.concatenate(
                [hi[:, rows], lo[:, rows], jnp.zeros((14, E), jnp.float32)], axis=0
            ).astype(jnp.bfloat16)

    weigh(3, 4, 4)
    for o in (7, 6, 5, 4):
        pack(o)
        if o == 4:
            near_copy(4).start()
        else:
            far_copy(o).start()
        if o == 7:
            far_copy(8).start()
    weigh(3, 0, 4)
    for o in (3, 2, 1, 0):
        pack(o)
        if o == 3:
            near_copy(3).start()

    k = kt[0, :E, :].astype(jnp.float32)
    sq = to_tile(jnp.sum(k * k, axis=0, keepdims=True))
    loglik[...] = LN2 * mine[x] - BETA * sq

    for r in range(2):
        far_copy(5 + r).wait_recv()
        far_copy(7 + r).wait_recv()
        for h in range(2):
            total = wsend[1 + r, h].astype(jnp.float32) + wnear[r, h].astype(jnp.float32)
            if h == r:
                total = total + wfar[r].astype(jnp.float32)
            mass = total[E : E + 1] + total[E + 1 : E + 2]
            hi = mass.astype(jnp.bfloat16).astype(jnp.float32)
            wsend[1 + r, h, :E, :] = total[:E].astype(jnp.bfloat16)
            wsend[1 + r, h, E:, :] = jnp.concatenate(
                [hi, mass - hi, jnp.zeros((14, E), jnp.float32)], axis=0
            ).astype(jnp.bfloat16)
        near_copy(1 + r).start()

    for o in (1, 2, 3, 4):
        near_copy(o).wait_recv()
    for h in range(2):
        total = wsend[0, h].astype(jnp.float32)
        for o in (1, 2, 3, 4):
            total = total + wrecv[o, h].astype(jnp.float32)
        mass = jnp.broadcast_to(total[E : E + 1] + total[E + 1 : E + 2], (E, E)).T
        rows = slice(h * E, (h + 1) * E)
        c = cb[0, rows, :E].astype(jnp.float32)
        new_code[rows, :] = ((total[:E] + c) / (mass + 1.0)).astype(jnp.bfloat16)

    for p in (1, 2, 3):
        key_copy(p, 0).wait_send()
        key_copy(p, 1).wait_send()
        core_copy(p).wait_send()
    for o in (1, 2, 3, 4):
        code_copy(o).wait_send()
        near_copy(o).wait_send()
    for o in (5, 6, 7, 8):
        pass_on(o).wait_send()
        far_copy(o).wait_send()
    for owner in range(NX):
        all_stats(owner).wait_send()


def local(keys, code):
    vmem = pl.BlockSpec(memory_space=pltpu.VMEM)
    hbm = pl.BlockSpec(memory_space=pl.ANY)
    bf16, f32 = jnp.bfloat16, jnp.float32
    dma = pltpu.SemaphoreType.DMA
    new_code, loglik = pl.pallas_call(
        kernel,
        out_shape=(
            jax.ShapeDtypeStruct((OWN, E), bf16),
            jax.ShapeDtypeStruct((8, TOK // 8), f32),
        ),
        in_specs=[hbm, hbm],
        out_specs=(vmem, vmem),
        scratch_shapes=[
            pltpu.VMEM((TOK, E), bf16),
            pltpu.VMEM((NX, 2 * E, TOK), bf16),
            pltpu.VMEM((NZ, OWN, 2 * E), bf16),
            pltpu.VMEM((NX * NZ, OWN, TOK), bf16),
            pltpu.VMEM((NX * NZ, 8, TOK), f32),
            pltpu.VMEM((NX * NZ, 8, TOK), f32),
            pltpu.VMEM((NX * NZ, 16, TOK), bf16),
            pltpu.VMEM((OWN, TOK), f32),
            pltpu.VMEM((OWN, TOK), f32),
            pltpu.VMEM((8, TOK), f32),
            pltpu.VMEM((8, TOK), f32),
            pltpu.VMEM((NX, 32, 8, TOK // 8), f32),
            pltpu.VMEM((NX, 8, TOK // 8), f32),
            pltpu.VMEM((NZ, OWN, 2 * E), f32),
            pltpu.VMEM((NZ, 2, HALF, E), bf16),
            pltpu.VMEM((2, 2, HALF, E), bf16),
            pltpu.VMEM((2, HALF, E), bf16),
            pltpu.VMEM((5, 2, HALF, E), bf16),
            dma((2,)),
            dma((2 * NX,)), dma((2 * NX,)), dma((NX,)), dma((NX,)),
            dma((NZ + 1,)), dma((NZ + 1,)),
            dma((NX,)), dma((NX,)), dma((NZ + 1,)), dma((NZ + 1,)),
        ],
        compiler_params=pltpu.CompilerParams(
            collective_id=0, has_side_effects=True, vmem_limit_bytes=62 * 2**20
        ),
    )(keys, code)
    return new_code, loglik.reshape(TOK)


def solution(mesh):
    return jax.shard_map(
        local,
        mesh=mesh,
        in_specs=(P("dp", None), P(("dp", "codebook"), None)),
        out_specs=(P(("dp", "codebook"), None), P("dp")),
        check_vma=False,
    )
```

time: 59.7 us -> 51.4 us (0.86)
  Pallas kernels: 55.9 us -> 48.6 us
  local copies, waits for them, and re-layouts: 3.01 us -> 2.07 us
    pallas_call x1, Pallas kernels: 55.9 us -> 48.6 us  [local(): pl.pallas_call(kernel, out_shape=(jax.ShapeDtypeStruct((OWN, E), bf16), j...]
    unnamed x6 -> x4, local copies, waits for them, and re-layouts: 3.01 us -> 2.07 us
where the time goes in v3:
time: 51.4 us; the launch traced here: 51.3 us
  Pallas kernels  48.6 us (95%)
  local copies, waits for them, and re-layouts  2.07 us (4%)
  between operations  0.65 us (1%)
    pallas_call x1, Pallas kernels, local(): pl.pallas_call(kernel, out_shape=(jax.ShapeDtypeStruct((OWN, E), bf16), j...  48.6 us
    unnamed x4, local copies, waits for them, and re-layouts  2.07 us

profile of v3, /device:TPU:1, one launch (start us, length us, event | category | flops | bytes accessed | tf_op | source)
XLA Modules:
  0.0 51.3 jit_solution(1237110871493520914)
XLA Ops:
  0.6 48.6 %shard_map.41 = (bf16[256,128]{1,0:T(8,128)(2,1)}, f32[8,128]{1,0:T(8,128)}) custom-call(bf16[1024,128]{1,0:T(8,128)(2,1)} %keys.1, bf16[256,128]{1,0:T(8,128)(2,1)} %code.1), custom_call_target="tpu_custom_call" | custom-call | tf_op jit(solution)/shard_map/pallas_call | solution.py:375
  49.2 0.0 copy-start
  49.2 1.5 %copy.6 = bf16[256,128]{1,0:T(8,128)(2,1)} copy(bf16[256,128]{1,0:T(8,128)(2,1)} %get-tuple-element.8) | data formatting | bytes 131072
  50.7 0.0 copy-done
  50.7 0.6 %copy.7 = f32[1024]{0:T(1024)} copy(f32[1024]{0:T(1024)S(1)} %bitcast.1) | data formatting | bytes 8192
Async XLA Ops:
  49.2 1.5 %copy-start = (f32[8,128]{1,0:T(8,128)S(1)}, f32[8,128]{1,0:T(8,128)}, u32[]{:S(2)}) copy-start(f32[8,128]{1,0:T(8,128)} %get-tuple-element.5) | copy-start | bytes 12292

commit v4 on v3

--- a/solution.py
+++ b/solution.py
@@ -28,7 +28,7 @@
 
 def kernel(
     keys, code, new_code, loglik,
-    raw, kt, cb, prob, top, tot, scale, s0, s1, x0, x1, stats, mine, acc, wsend, wnear, wfar, wrecv,
+    raw, kt, cb, prob, top, tot, scale, score, high, stats, mine, acc, wsend, wnear, wfar, wrecv,
     in_sem, key_send, key_recv, core_send, core_recv, code_send, code_recv,
     stat_send, stat_recv, sum_send, sum_recv,
 ):
@@ -115,12 +115,15 @@
     pl.semaphore_wait(barrier, len(others) + NZ - 1)
     for p, h in ((1, 1), (2, 0), (1, 0), (2, 1)):
         key_copy(p, h).start()
-    for o in (1, 2, 3, 4):
+    for o in (1, 2):
         code_copy(o).start()
 
     def place(u):
-        near_i = (u + 27) // 32 + (u + 22) // 32
-        near_o = u - 5 * near_i
+        late = (u + 23) // 32
+        v = u - 9 * late
+        n3 = v // 3
+        near_i = (1 - late) * n3 + late * (v - 3 * n3)
+        near_o = (1 - late) * (v - 3 * n3) + late * (3 + n3)
         far = (u + 17) // 32
         t = u - 15
         opposite = (x + 2) & 3
@@ -135,30 +138,22 @@
         far_o = (1 - b) * (5 + t - 3 * n1) + (b - c) * t1 + c * (5 + t2 - 3 * n2)
         return (1 - far) * near_i + far * far_i, (1 - far) * near_o + far * far_o
 
-    def cross(u, s, m):
+    spans = [slice(q * TILE, (q + 1) * TILE) for q in range(TOK // TILE)]
+
+    def cross(u, span):
         i, o = place(u)
-        for q in range(TOK // TILE):
-            span = slice(q * TILE, (q + 1) * TILE)
-            v = jnp.dot(cb[o], kt[i, :, span], preferred_element_type=jnp.float32)
-            s[:, span] = v
-            m[:, span] = jnp.max(v.reshape(OWN // 8, 8, TILE), axis=0)
-            yield
-
-    def power(u, s, m):
+        v = jnp.dot(cb[o], kt[i, :, span], preferred_element_type=jnp.float32)
+        score[:, span] = v
+        high[:, span] = jnp.max(v.reshape(OWN // 8, 8, TILE), axis=0)
+
+    def power(u, span):
         i, o = place(u)
         k = i * NZ + o
-        for q in range(TOK // TILE):
-            span = slice(q * TILE, (q + 1) * TILE)
-            peak = jnp.max(m[:, span], axis=0, keepdims=True)
-            p = jnp.exp2((s[:, span] - peak) * ALPHA)
-            top[k, :, span] = jnp.broadcast_to(peak, (8, TILE))
-            tot[k, :, span] = jnp.sum(p.reshape(OWN // 8, 8, TILE), axis=0)
-            prob[k, :, span] = p.astype(jnp.bfloat16)
-            yield
-
-    def both(u, later, now):
-        for _ in zip(cross(u + 1, *later), power(u, *now)):
-            pass
+        peak = jnp.max(high[:, span], axis=0, keepdims=True)
+        p = jnp.exp2((score[:, span] - peak) * ALPHA)
+        top[k, :, span] = jnp.broadcast_to(peak, (8, TILE))
+        tot[k, :, span] = jnp.sum(p.reshape(OWN // 8, 8, TILE), axis=0)
+        prob[k, :, span] = p.astype(jnp.bfloat16)
 
     def all_stats(owner):
         return remote(
@@ -214,36 +209,47 @@
             pass_on(8).wait_recv()
         prepare(o)
 
-    turn = ((s0, x0), (s1, x1))
-
     def steps(u, n):
         for j in range(n):
-            both(u + j, turn[(j + 1) % 2], turn[j % 2])
-
-    for _ in cross(0, *turn[0]):
-        pass
-    need_code(1)
-    need_code(2)
+            for span in spans:
+                power(u + j, span)
+                cross(u + j + 1, span)
+
+    for span in spans:
+        cross(0, span)
     for p, h in ((1, 1), (2, 0)):
         key_copy(p, h).wait_recv()
         key_copy(3, h).start()
+    for o in (3, 4):
+        code_copy(o).start()
+    need_code(1)
+    need_code(2)
     for p, h in ((1, 0), (2, 1)):
         key_copy(p, h).wait_recv()
         core_copy(p).start()
-    need_code(3)
-    need_code(4)
+    steps(0, 2)
 
     def near(n, carry):
-        for p in (1, 2):
-            on(n, p)(lambda p=p: core_copy(p).wait_recv())
-        steps(4 * n, 4)
+        @on(n, 0)
+        def _():
+            core_copy(1).wait_recv()
+            core_copy(2).wait_recv()
+
+        @on(n, 1)
+        def _():
+            need_code(3)
+            need_code(4)
+
+        @on(n, 2)
+        def _():
+            key_copy(3, 0).wait_recv()
+            key_copy(3, 1).wait_recv()
+            core_copy(3).start()
+
+        steps(2 + 4 * n, 4)
         return carry
 
     lax.fori_loop(0, 3, near, 0)
-    key_copy(3, 0).wait_recv()
-    key_copy(3, 1).wait_recv()
-    core_copy(3).start()
-    steps(12, 2)
     for o in (5, 6, 7):
         need_code(o)
     core_copy(3).wait_recv()
@@ -261,9 +267,9 @@
         return carry
 
     lax.fori_loop(0, 4, far, 0)
-    both(30, turn[1], turn[0])
-    for _ in power(31, *turn[1]):
-        pass
+    steps(30, 1)
+    for span in spans:
+        power(31, span)
     send_stats(3)
 
     def weigh(owner, o, m):
@@ -282,18 +288,15 @@
     lax.fori_loop(0, 3, shard, 0)
     finish_stats(3)
 
-    def far_copy(o):
-        src, dst, dz = (
-            (wsend.at[5], wnear.at[0], 1),
-            (wsend.at[6], wnear.at[1], -1),
-            (wsend.at[7, 0], wfar.at[0], 2),
-            (wsend.at[7, 1], wfar.at[1], -2),
-        )[o - 5]
-        return remote(src, dst, sum_send.at[o], sum_recv.at[o], at(dz=dz))
-
-    def near_copy(o):
-        return remote(
-            wsend.at[o], wrecv.at[o], sum_send.at[o], sum_recv.at[o], at(dz=CODE_AT[o])
+    def far_copy(o, h):
+        dst, dz = {5: (wnear.at[0, h], 1), 6: (wnear.at[1, h], -1), 7: (wfar.at[h], 2 - 4 * h)}[o]
+        k = 2 * o + h
+        return remote(wsend.at[o, h], dst, sum_send.at[k], sum_recv.at[k], at(dz=dz))
+
+    def near_copy(o, h):
+        k = 2 * o + h
+        return remote(
+            wsend.at[o, h], wrecv.at[o, h], sum_send.at[k], sum_recv.at[k], at(dz=CODE_AT[o])
         )
 
     def pack(o):
@@ -308,42 +311,47 @@
                 [hi[:, rows], lo[:, rows], jnp.zeros((14, E), jnp.float32)], axis=0
             ).astype(jnp.bfloat16)
 
-    weigh(3, 4, 4)
-    for o in (7, 6, 5, 4):
+    weigh(3, 5, 3)
+    pack(5)
+    pack(6)
+    far_copy(5, 1).start()
+    far_copy(6, 0).start()
+    pack(7)
+    for o, h in ((7, 0), (7, 1), (5, 0), (6, 1)):
+        far_copy(o, h).start()
+    weigh(3, 0, 5)
+    for o in (1, 2, 3, 4, 0):
         pack(o)
-        if o == 4:
-            near_copy(4).start()
-        else:
-            far_copy(o).start()
-        if o == 7:
-            far_copy(8).start()
-    weigh(3, 0, 4)
-    for o in (3, 2, 1, 0):
-        pack(o)
-        if o == 3:
-            near_copy(3).start()
 
     k = kt[0, :E, :].astype(jnp.float32)
     sq = to_tile(jnp.sum(k * k, axis=0, keepdims=True))
     loglik[...] = LN2 * mine[x] - BETA * sq
 
-    for r in range(2):
-        far_copy(5 + r).wait_recv()
-        far_copy(7 + r).wait_recv()
+    def relay(r, h):
+        far_copy(5 + r, h).wait_recv()
+        total = wsend[1 + r, h].astype(jnp.float32) + wnear[r, h].astype(jnp.float32)
+        if h == r:
+            far_copy(7, h).wait_recv()
+            total = total + wfar[r].astype(jnp.float32)
+        mass = total[E : E + 1] + total[E + 1 : E + 2]
+        hi = mass.astype(jnp.bfloat16).astype(jnp.float32)
+        wsend[1 + r, h, :E, :] = total[:E].astype(jnp.bfloat16)
+        wsend[1 + r, h, E:, :] = jnp.concatenate(
+            [hi, mass - hi, jnp.zeros((14, E), jnp.float32)], axis=0
+        ).astype(jnp.bfloat16)
+        near_copy(1 + r, h).start()
+
+    relay(0, 1)
+    relay(1, 0)
+    for o in (3, 4):
         for h in range(2):
-            total = wsend[1 + r, h].astype(jnp.float32) + wnear[r, h].astype(jnp.float32)
-            if h == r:
-                total = total + wfar[r].astype(jnp.float32)
-            mass = total[E : E + 1] + total[E + 1 : E + 2]
-            hi = mass.astype(jnp.bfloat16).astype(jnp.float32)
-            wsend[1 + r, h, :E, :] = total[:E].astype(jnp.bfloat16)
-            wsend[1 + r, h, E:, :] = jnp.concatenate(
-                [hi, mass - hi, jnp.zeros((14, E), jnp.float32)], axis=0
-            ).astype(jnp.bfloat16)
-        near_copy(1 + r).start()
-
-    for o in (1, 2, 3, 4):
-        near_copy(o).wait_recv()
+            near_copy(o, h).start()
+    relay(0, 0)
+    relay(1, 1)
+
+    for o in (3, 4, 1, 2):
+        for h in range(2):
+            near_copy(o, h).wait_recv()
     for h in range(2):
         total = wsend[0, h].astype(jnp.float32)
         for o in (1, 2, 3, 4):
@@ -359,10 +367,13 @@
         core_copy(p).wait_send()
     for o in (1, 2, 3, 4):
         code_copy(o).wait_send()
-        near_copy(o).wait_send()
+        near_copy(o, 0).wait_send()
+        near_copy(o, 1).wait_send()
     for o in (5, 6, 7, 8):
         pass_on(o).wait_send()
-        far_copy(o).wait_send()
+    for o in (5, 6, 7):
+        far_copy(o, 0).wait_send()
+        far_copy(o, 1).wait_send()
     for owner in range(NX):
         all_stats(owner).wait_send()
 
@@ -389,8 +400,6 @@
             pltpu.VMEM((NX * NZ, 8, TOK), f32),
             pltpu.VMEM((NX * NZ, 16, TOK), bf16),
             pltpu.VMEM((OWN, TOK), f32),
-            pltpu.VMEM((OWN, TOK), f32),
-            pltpu.VMEM((8, TOK), f32),
             pltpu.VMEM((8, TOK), f32),
             pltpu.VMEM((NX, 32, 8, TOK // 8), f32),
             pltpu.VMEM((NX, 8, TOK // 8), f32),
@@ -402,7 +411,7 @@
             dma((2,)),
             dma((2 * NX,)), dma((2 * NX,)), dma((NX,)), dma((NX,)),
             dma((NZ + 1,)), dma((NZ + 1,)),
-            dma((NX,)), dma((NX,)), dma((NZ + 1,)), dma((NZ + 1,)),
+            dma((NX,)), dma((NX,)), dma((2 * NZ,)), dma((2 * NZ,)),
         ],
         compiler_params=pltpu.CompilerParams(
             collective_id=0, has_side_effects=True, vmem_limit_bytes=62 * 2**20

time: 51.4 us -> 50.2 us (0.977)
  Pallas kernels: 48.6 us -> 47.4 us
    pallas_call x1, Pallas kernels: 48.6 us -> 47.4 us  [local(): pl.pallas_call(kernel, out_shape=(jax.ShapeDtypeStruct((OWN, E), bf16), j...]
where the time goes in v4:
time: 50.2 us; the launch traced here: 50.1 us
  Pallas kernels  47.4 us (94%)
  local copies, waits for them, and re-layouts  2.07 us (4%)
  between operations  0.65 us (1%)
    pallas_call x1, Pallas kernels, local(): pl.pallas_call(kernel, out_shape=(jax.ShapeDtypeStruct((OWN, E), bf16), j...  47.4 us
    unnamed x4, local copies, waits for them, and re-layouts  2.07 us

profile of v4, /device:TPU:1, one launch (start us, length us, event | category | flops | bytes accessed | tf_op | source)
XLA Modules:
  0.0 50.1 jit_solution(13409172958878094380)
XLA Ops:
  0.6 47.4 %shard_map.41 = (bf16[256,128]{1,0:T(8,128)(2,1)}, f32[8,128]{1,0:T(8,128)}) custom-call(bf16[1024,128]{1,0:T(8,128)(2,1)} %keys.1, bf16[256,128]{1,0:T(8,128)(2,1)} %code.1), custom_call_target="tpu_custom_call" | custom-call | tf_op jit(solution)/shard_map/pallas_call | solution.py:386
  48.0 0.0 copy-start
  48.0 1.5 %copy.6 = bf16[256,128]{1,0:T(8,128)(2,1)} copy(bf16[256,128]{1,0:T(8,128)(2,1)} %get-tuple-element.8) | data formatting | bytes 131072
  49.5 0.0 copy-done
  49.5 0.6 %copy.7 = f32[1024]{0:T(1024)} copy(f32[1024]{0:T(1024)S(1)} %bitcast.1) | data formatting | bytes 8192
Async XLA Ops:
  48.0 1.5 %copy-start = (f32[8,128]{1,0:T(8,128)S(1)}, f32[8,128]{1,0:T(8,128)}, u32[]{:S(2)}) copy-start(f32[8,128]{1,0:T(8,128)} %get-tuple-element.5) | copy-start | bytes 12292

commit v5 on v4

--- a/solution.py
+++ b/solution.py
@@ -30,7 +30,7 @@
     keys, code, new_code, loglik,
     raw, kt, cb, prob, top, tot, scale, score, high, stats, mine, acc, wsend, wnear, wfar, wrecv,
     in_sem, key_send, key_recv, core_send, core_recv, code_send, code_recv,
-    stat_send, stat_recv, sum_send, sum_recv,
+    stat_send, stat_recv, sum_send, sum_recv, met,
 ):
     dp, col = lax.axis_index("dp"), lax.axis_index("codebook")
     x, z = dp >> 3, dp & 7
@@ -44,22 +44,19 @@
 
     others = [(dx, dy, dc) for dx in range(4) for dy in range(4) for dc in range(2)][1:]
 
+    column = [(dy, dc) for dy in range(4) for dc in range(2)][1:]
+    close = [at(dz=d) for d in (2, -2, 1, -1)] + [at(dx=d) for d in (2, 1, -1)]
+    close += [at(dy=dy, dc=dc) for dy, dc in column]
     barrier = pltpu.get_barrier_semaphore()
-    for dz in range(1, NZ):
-        pl.semaphore_signal(barrier, inc=1, device_id=at(dz=dz), device_id_type=MESH)
-    for dx, dy, dc in others:
-        pl.semaphore_signal(
-            barrier, inc=1, device_id=at(dx=dx, dy=dy, dc=dc), device_id_type=MESH
-        )
+    for to in close:
+        pl.semaphore_signal(barrier, inc=1, device_id=to, device_id_type=MESH)
 
     get_code = pltpu.make_async_copy(code, cb.at[0, :, :E], in_sem.at[0])
     get_keys = pltpu.make_async_copy(keys, raw, in_sem.at[1])
     get_keys.start()
     get_code.start()
-    row = lax.broadcasted_iota(jnp.int32, (E, TOK), 0)
-    ones = jnp.where(row < 3, 1.0, 0.0).astype(jnp.bfloat16)
     for i in range(NX):
-        kt[i, E:, :] = ones
+        kt[i, E:, :] = jnp.ones((E, TOK), jnp.bfloat16)
     acc[...] = jnp.zeros_like(acc)
     get_keys.wait()
     kt[0, :E, :] = raw[...].astype(jnp.float32).T.astype(jnp.bfloat16)
@@ -112,7 +109,7 @@
         cb[o, :, E:] = jnp.where(lane < 3, both, 0.0).astype(jnp.bfloat16)
 
     prepare(0)
-    pl.semaphore_wait(barrier, len(others) + NZ - 1)
+    pl.semaphore_wait(barrier, len(close))
     for p, h in ((1, 1), (2, 0), (1, 0), (2, 1)):
         key_copy(p, h).start()
     for o in (1, 2):
@@ -217,6 +214,8 @@
 
     for span in spans:
         cross(0, span)
+    for dx in (2, 1, -1):
+        pl.semaphore_signal(met, inc=1, device_id=at(dx=dx), device_id_type=MESH)
     for p, h in ((1, 1), (2, 0)):
         key_copy(p, h).wait_recv()
         key_copy(3, h).start()
@@ -254,20 +253,20 @@
         need_code(o)
     core_copy(3).wait_recv()
 
-    def done(owner):
-        opposite = (x + 2) & 3
-        return 17 + 3 * owner + 5 * ((owner - opposite + 4) >> 2)
+    pl.semaphore_wait(met, 3)
 
     def far(n, carry):
-        u = 14 + 4 * n
-        steps(u, 4)
-        for owner in range(3):
-            when = (done(owner) - 14) >> 2
-            on(n, when)(lambda owner=owner: send_stats(owner))
+        steps(14 + 4 * n, 4)
         return carry
 
-    lax.fori_loop(0, 4, far, 0)
-    steps(30, 1)
+    lax.fori_loop(0, 2, far, 0)
+    steps(22, 1)
+    send_stats(0)
+    steps(23, 3)
+    send_stats(1)
+    steps(26, 3)
+    send_stats(2)
+    steps(29, 2)
     for span in spans:
         power(31, span)
     send_stats(3)
@@ -299,16 +298,19 @@
             wsend.at[o, h], wrecv.at[o, h], sum_send.at[k], sum_recv.at[k], at(dz=CODE_AT[o])
         )
 
+    diagonal = lax.broadcasted_iota(jnp.int32, (E, E), 0) == lax.broadcasted_iota(
+        jnp.int32, (E, E), 1
+    )
+
     def pack(o):
         w = acc[o]
-        mass = w[:, E:].T[0:1, :]
-        hi = mass.astype(jnp.bfloat16).astype(jnp.float32)
-        lo = mass - hi
         for h in range(2):
             rows = slice(h * E, (h + 1) * E)
             wsend[o, h, :E, :] = w[rows, :E].astype(jnp.bfloat16)
+            mass = jnp.sum(jnp.where(diagonal, w[rows, E:], 0.0), axis=0, keepdims=True)
+            hi = mass.astype(jnp.bfloat16).astype(jnp.float32)
             wsend[o, h, E:, :] = jnp.concatenate(
-                [hi[:, rows], lo[:, rows], jnp.zeros((14, E), jnp.float32)], axis=0
+                [hi, mass - hi, jnp.zeros((14, E), jnp.float32)], axis=0
             ).astype(jnp.bfloat16)
 
     weigh(3, 5, 3)
@@ -412,6 +414,7 @@
             dma((2 * NX,)), dma((2 * NX,)), dma((NX,)), dma((NX,)),
             dma((NZ + 1,)), dma((NZ + 1,)),
             dma((NX,)), dma((NX,)), dma((2 * NZ,)), dma((2 * NZ,)),
+            pltpu.SemaphoreType.REGULAR,
         ],
         compiler_params=pltpu.CompilerParams(
             collective_id=0, has_side_effects=True, vmem_limit_bytes=62 * 2**20

time: 50.2 us -> 48.3 us (0.962)
  Pallas kernels: 47.4 us -> 45.4 us
    pallas_call x1, Pallas kernels: 47.4 us -> 45.4 us  [local(): pl.pallas_call(kernel, out_shape=(jax.ShapeDtypeStruct((OWN, E), bf16), j...]
where the time goes in v5:
time: 48.3 us; the launch traced here: 48.2 us
  Pallas kernels  45.4 us (94%)
  local copies, waits for them, and re-layouts  2.07 us (4%)
  between operations  0.65 us (1%)
    pallas_call x1, Pallas kernels, local(): pl.pallas_call(kernel, out_shape=(jax.ShapeDtypeStruct((OWN, E), bf16), j...  45.4 us
    unnamed x4, local copies, waits for them, and re-layouts  2.07 us

profile of v5, /device:TPU:1, one launch (start us, length us, event | category | flops | bytes accessed | tf_op | source)
XLA Modules:
  0.0 48.2 jit_solution(15672321124231562381)
XLA Ops:
  0.6 45.4 %shard_map.41 = (bf16[256,128]{1,0:T(8,128)(2,1)}, f32[8,128]{1,0:T(8,128)}) custom-call(bf16[1024,128]{1,0:T(8,128)(2,1)} %keys.1, bf16[256,128]{1,0:T(8,128)(2,1)} %code.1), custom_call_target="tpu_custom_call" | custom-call | tf_op jit(solution)/shard_map/pallas_call | solution.py:388
  46.1 0.0 copy-start
  46.1 1.5 %copy.6 = bf16[256,128]{1,0:T(8,128)(2,1)} copy(bf16[256,128]{1,0:T(8,128)(2,1)} %get-tuple-element.8) | data formatting | bytes 131072
  47.6 0.0 copy-done
  47.6 0.6 %copy.7 = f32[1024]{0:T(1024)} copy(f32[1024]{0:T(1024)S(1)} %bitcast.1) | data formatting | bytes 8192
Async XLA Ops:
  46.1 1.5 %copy-start = (f32[8,128]{1,0:T(8,128)S(1)}, f32[8,128]{1,0:T(8,128)}, u32[]{:S(2)}) copy-start(f32[8,128]{1,0:T(8,128)} %get-tuple-element.5) | copy-start | bytes 12292

commit v6 on v5

--- a/solution.py
+++ b/solution.py
@@ -44,6 +44,11 @@
 
     others = [(dx, dy, dc) for dx in range(4) for dy in range(4) for dc in range(2)][1:]
 
+    get_code = pltpu.make_async_copy(code, cb.at[0, :, :E], in_sem.at[0])
+    get_keys = pltpu.make_async_copy(keys, raw, in_sem.at[1])
+    get_keys.start()
+    get_code.start()
+
     column = [(dy, dc) for dy in range(4) for dc in range(2)][1:]
     close = [at(dz=d) for d in (2, -2, 1, -1)] + [at(dx=d) for d in (2, 1, -1)]
     close += [at(dy=dy, dc=dc) for dy, dc in column]
@@ -51,21 +56,12 @@
     for to in close:
         pl.semaphore_signal(barrier, inc=1, device_id=to, device_id_type=MESH)
 
-    get_code = pltpu.make_async_copy(code, cb.at[0, :, :E], in_sem.at[0])
-    get_keys = pltpu.make_async_copy(keys, raw, in_sem.at[1])
-    get_keys.start()
-    get_code.start()
-    for i in range(NX):
-        kt[i, E:, :] = jnp.ones((E, TOK), jnp.bfloat16)
-    acc[...] = jnp.zeros_like(acc)
     get_keys.wait()
     kt[0, :E, :] = raw[...].astype(jnp.float32).T.astype(jnp.bfloat16)
     get_code.wait()
 
     def quarter(h):
         return pl.ds(pl.multiple_of(core * (E // 2) + h * (E // 4), E // 4), E // 4)
-
-    half = pl.ds(pl.multiple_of(core * (E // 2), E // 2), E // 2)
 
     def remote(src, dst, send, recv, to):
         return pltpu.make_async_remote_copy(
@@ -81,9 +77,10 @@
             key_send.at[2 * p + h], key_recv.at[2 * p + h], at(dx=dx),
         )
 
-    def core_copy(p):
-        return remote(
-            kt.at[p, half], kt.at[p, half], core_send.at[p], core_recv.at[p], at(dc=1)
+    def core_copy(p, h):
+        k = 2 * p + h
+        return remote(
+            kt.at[p, quarter(h)], kt.at[p, quarter(h)], core_send.at[k], core_recv.at[k], at(dc=1)
         )
 
     def code_copy(o):
@@ -108,12 +105,17 @@
         both = jnp.where(lane == 0, hi, jnp.where(lane == 1, mid, lo))
         cb[o, :, E:] = jnp.where(lane < 3, both, 0.0).astype(jnp.bfloat16)
 
-    prepare(0)
     pl.semaphore_wait(barrier, len(close))
     for p, h in ((1, 1), (2, 0), (1, 0), (2, 1)):
         key_copy(p, h).start()
     for o in (1, 2):
         code_copy(o).start()
+    for dx in (2, 1, -1):
+        pl.semaphore_signal(met, inc=1, device_id=at(dx=dx), device_id_type=MESH)
+    for i in range(NX):
+        kt[i, E:, :] = jnp.ones((E, TOK), jnp.bfloat16)
+    acc[...] = jnp.zeros_like(acc)
+    prepare(0)
 
     def place(u):
         late = (u + 23) // 32
@@ -214,25 +216,25 @@
 
     for span in spans:
         cross(0, span)
-    for dx in (2, 1, -1):
-        pl.semaphore_signal(met, inc=1, device_id=at(dx=dx), device_id_type=MESH)
     for p, h in ((1, 1), (2, 0)):
         key_copy(p, h).wait_recv()
         key_copy(3, h).start()
+        core_copy(p, h).start()
     for o in (3, 4):
         code_copy(o).start()
     need_code(1)
     need_code(2)
     for p, h in ((1, 0), (2, 1)):
         key_copy(p, h).wait_recv()
-        core_copy(p).start()
+        core_copy(p, h).start()
     steps(0, 2)
 
     def near(n, carry):
         @on(n, 0)
         def _():
-            core_copy(1).wait_recv()
-            core_copy(2).wait_recv()
+            for p in (1, 2):
+                core_copy(p, 0).wait_recv()
+                core_copy(p, 1).wait_recv()
 
         @on(n, 1)
         def _():
@@ -241,18 +243,19 @@
 
         @on(n, 2)
         def _():
-            key_copy(3, 0).wait_recv()
-            key_copy(3, 1).wait_recv()
-            core_copy(3).start()
+            for h in range(2):
+                key_copy(3, h).wait_recv()
+                core_copy(3, h).start()
 
         steps(2 + 4 * n, 4)
         return carry
 
     lax.fori_loop(0, 3, near, 0)
-    for o in (5, 6, 7):
-        need_code(o)
-    core_copy(3).wait_recv()
-
+    need_code(5)
+    need_code(6)
+    core_copy(3, 0).wait_recv()
+    core_copy(3, 1).wait_recv()
+    need_code(7)
     pl.semaphore_wait(met, 3)
 
     def far(n, carry):
@@ -262,11 +265,10 @@
     lax.fori_loop(0, 2, far, 0)
     steps(22, 1)
     send_stats(0)
-    steps(23, 3)
+    steps(23, 4)
     send_stats(1)
-    steps(26, 3)
+    steps(27, 4)
     send_stats(2)
-    steps(29, 2)
     for span in spans:
         power(31, span)
     send_stats(3)
@@ -366,7 +368,8 @@
     for p in (1, 2, 3):
         key_copy(p, 0).wait_send()
         key_copy(p, 1).wait_send()
-        core_copy(p).wait_send()
+        core_copy(p, 0).wait_send()
+        core_copy(p, 1).wait_send()
     for o in (1, 2, 3, 4):
         code_copy(o).wait_send()
         near_copy(o, 0).wait_send()
@@ -411,7 +414,7 @@
             pltpu.VMEM((2, HALF, E), bf16),
             pltpu.VMEM((5, 2, HALF, E), bf16),
             dma((2,)),
-            dma((2 * NX,)), dma((2 * NX,)), dma((NX,)), dma((NX,)),
+            dma((2 * NX,)), dma((2 * NX,)), dma((2 * NX,)), dma((2 * NX,)),
             dma((NZ + 1,)), dma((NZ + 1,)),
             dma((NX,)), dma((NX,)), dma((2 * NZ,)), dma((2 * NZ,)),
             pltpu.SemaphoreType.REGULAR,

time: 48.3 us -> 48.2 us (level)
  no operation moved by 1% of the time
where the time goes in v6:
time: 48.2 us; the launch traced here: 48.1 us
  Pallas kernels  45.3 us (94%)
  local copies, waits for them, and re-layouts  2.07 us (4%)
  between operations  0.65 us (1%)
    pallas_call x1, Pallas kernels, local(): pl.pallas_call(kernel, out_shape=(jax.ShapeDtypeStruct((OWN, E), bf16), j...  45.3 us
    unnamed x4, local copies, waits for them, and re-layouts  2.07 us

profile of v6, /device:TPU:1, one launch (start us, length us, event | category | flops | bytes accessed | tf_op | source)
XLA Modules:
  0.0 48.1 jit_solution(6137803357424835097)
XLA Ops:
  0.6 45.3 %shard_map.41 = (bf16[256,128]{1,0:T(8,128)(2,1)}, f32[8,128]{1,0:T(8,128)}) custom-call(bf16[1024,128]{1,0:T(8,128)(2,1)} %keys.1, bf16[256,128]{1,0:T(8,128)(2,1)} %code.1), custom_call_target="tpu_custom_call" | custom-call | tf_op jit(solution)/shard_map/pallas_call | solution.py:391
  46.0 0.0 copy-start
  46.0 1.5 %copy.6 = bf16[256,128]{1,0:T(8,128)(2,1)} copy(bf16[256,128]{1,0:T(8,128)(2,1)} %get-tuple-element.8) | data formatting | bytes 131072
  47.5 0.0 copy-done
  47.5 0.6 %copy.7 = f32[1024]{0:T(1024)} copy(f32[1024]{0:T(1024)S(1)} %bitcast.1) | data formatting | bytes 8192
Async XLA Ops:
  46.0 1.5 %copy-start = (f32[8,128]{1,0:T(8,128)S(1)}, f32[8,128]{1,0:T(8,128)}, u32[]{:S(2)}) copy-start(f32[8,128]{1,0:T(8,128)} %get-tuple-element.5) | copy-start | bytes 12292

commit v7 on v6

--- a/solution.py
+++ b/solution.py
@@ -316,12 +316,12 @@
             ).astype(jnp.bfloat16)
 
     weigh(3, 5, 3)
+    pack(7)
+    far_copy(7, 0).start()
+    far_copy(7, 1).start()
     pack(5)
     pack(6)
-    far_copy(5, 1).start()
-    far_copy(6, 0).start()
-    pack(7)
-    for o, h in ((7, 0), (7, 1), (5, 0), (6, 1)):
+    for o, h in ((5, 1), (6, 0), (5, 0), (6, 1)):
         far_copy(o, h).start()
     weigh(3, 0, 5)
     for o in (1, 2, 3, 4, 0):

time: 48.2 us -> 48.7 us (1.010)
  no operation moved by 1% of the time
where the time goes in v7:
time: 48.7 us; the launch traced here: 48.4 us
  Pallas kernels  45.7 us (94%)
  local copies, waits for them, and re-layouts  2.07 us (4%)
  between operations  0.65 us (1%)
    pallas_call x1, Pallas kernels, local(): pl.pallas_call(kernel, out_shape=(jax.ShapeDtypeStruct((OWN, E), bf16), j...  45.7 us
    unnamed x4, local copies, waits for them, and re-layouts  2.07 us

profile of v7, /device:TPU:1, one launch (start us, length us, event | category | flops | bytes accessed | tf_op | source)
XLA Modules:
  0.0 48.4 jit_solution(1438929098907278398)
XLA Ops:
  0.6 45.7 %shard_map.41 = (bf16[256,128]{1,0:T(8,128)(2,1)}, f32[8,128]{1,0:T(8,128)}) custom-call(bf16[1024,128]{1,0:T(8,128)(2,1)} %keys.1, bf16[256,128]{1,0:T(8,128)(2,1)} %code.1), custom_call_target="tpu_custom_call" | custom-call | tf_op jit(solution)/shard_map/pallas_call | solution.py:391
  46.3 0.0 copy-start
  46.3 1.5 %copy.6 = bf16[256,128]{1,0:T(8,128)(2,1)} copy(bf16[256,128]{1,0:T(8,128)(2,1)} %get-tuple-element.8) | data formatting | bytes 131072
  47.8 0.0 copy-done
  47.8 0.6 %copy.7 = f32[1024]{0:T(1024)} copy(f32[1024]{0:T(1024)S(1)} %bitcast.1) | data formatting | bytes 8192
Async XLA Ops:
  46.3 1.5 %copy-start = (f32[8,128]{1,0:T(8,128)S(1)}, f32[8,128]{1,0:T(8,128)}, u32[]{:S(2)}) copy-start(f32[8,128]{1,0:T(8,128)} %get-tuple-element.5) | copy-start | bytes 12292
